TPU v7x, 256 devices: a whole 4x4x8 slice. The times are simulated.
256 devices in a mesh: gx: 32 (over x, z_hi, core), gy: 8 (over y, z_lo).
Axes of the slice: x: 4, y: 4, z: 8 (z_hi: 4, z_lo: 2; z = z_hi * 2 + z_lo), core: 2. Of those that a mesh axis runs over, the one named last changes fastest.
Arguments:
- populations: float32 [19, 256, 128, 128], P(None, 'gx', 'gy'), may hold values from 0.0097 to 0.5, as said below
- cell_flags: int32 [4, 256, 128, 128], P(None, 'gx', 'gy'), may hold values from 0 to 3, as said below
- fill_level: float32 [256, 128, 128], P('gx', 'gy'), may hold values from 0.05 to 0.95
- tile_block: int32 [64, 8], P('gx', 'gy'), may hold values from 0 to 255, as said below
- deck_weights: bfloat16 [64, 8, 64, 1024], P('gx', 'gy'), may hold values from -1.5 to 1.5
Outputs:
- final_populations: float32 [19, 256, 128, 128], P(None, 'gx', 'gy')
- mass_change: float32 [256, 128, 128], P('gx', 'gy')
- shell_loads: float32 [256, 4, 1024], P(('gx', 'gy'))
Inputs may be any that keep to these rules, and one draw needn't show every extreme that they name: `cell_flags`: 0 fluid, 1 interface, 2 gas, 3 wall. `tile_block`: every block is named by exactly 2 tiles. `populations`: each population is its lattice weight times a factor between 0.35 and 1.65.
All inputs are finite; a program needn't handle non-finite values.
Results may differ from a plain program's by a relative error of at most 0.0029.
Values sent between devices are 32-bit elements; how exact they have to be, the bound alone decides.
A program may use at most 192 MiB of HBM per device.

v0:
```python
import jax
import jax.numpy as jnp
from jax import lax
from jax.sharding import PartitionSpec as P

velocity_table = (
    (0, 0, 0),
    (1, 0, 0),
    (-1, 0, 0),
    (0, 1, 0),
    (0, -1, 0),
    (0, 0, 1),
    (0, 0, -1),
    (1, 1, 0),
    (-1, -1, 0),
    (1, -1, 0),
    (-1, 1, 0),
    (1, 0, 1),
    (-1, 0, -1),
    (1, 0, -1),
    (-1, 0, 1),
    (0, 1, 1),
    (0, -1, -1),
    (0, 1, -1),
    (0, -1, 1),
)
weight_table = (1.0 / 3.0,) + (1.0 / 18.0,) * 6 + (1.0 / 36.0,) * 12
opposite_index = (0, 2, 1, 4, 3, 6, 5, 8, 7, 10, 9, 12, 11, 14, 13, 16, 15, 18, 17)
relax_time = 0.8
gravity = 0.001


def with_halo(block, sides, width):
    for axis, dim in sides:
        count = lax.axis_size(axis)
        forward = [(i, i + 1) for i in range(count - 1)]
        backward = [(target, source) for source, target in forward]
        low = lax.ppermute(
            lax.slice_in_dim(block, block.shape[dim] - width, None, axis=dim), axis, forward
        )
        high = lax.ppermute(lax.slice_in_dim(block, 0, width, axis=dim), axis, backward)
        block = jnp.concatenate([low, block, high], axis=dim)
    return block


def project_onto(component, vector):
    result = None
    for dimension in range(3):
        factor = velocity_table[component][dimension]
        if factor != 0:
            addend = float(factor) * vector[dimension]
            result = addend if result is None else result + addend
    return result


def momentum(values_in):
    totals = []
    for dimension in range(3):
        summed = None
        for component in range(19):
            factor = velocity_table[component][dimension]
            if factor != 0:
                addend = float(factor) * values_in[component]
                summed = addend if summed is None else summed + addend
        totals.append(summed)
    return totals


def phase_of(cell_flag, fill_level):
    return jnp.where(
        cell_flag == 0,
        1.0,
        jnp.where(cell_flag == 1, fill_level, jnp.where(cell_flag == 2, 0.0, -1.0)),
    )


def pad_depth(block):
    plane_shape = block.shape[:3] + (1,)
    below = jnp.zeros(plane_shape, jnp.float32).at[19].set(-1.0)
    above = jnp.zeros(plane_shape, jnp.float32)
    return jnp.concatenate([below, block, above], axis=3)


def advance(padded, resident, fill_level, cell_flag):
    cells_x, cells_y, cells_z = (resident.shape[1], resident.shape[2], resident.shape[3])
    current = momentum(resident)
    speed_square = current[0] * current[0] + current[1] * current[1] + current[2] * current[2]
    read = [resident[0]]
    exchanged = jnp.zeros(resident.shape[1:], jnp.float32)
    for component in range(1, 19):
        shift_x, shift_y, shift_z = velocity_table[component]
        pulled = padded[
            component,
            1 - shift_x : 1 - shift_x + cells_x,
            1 - shift_y : 1 - shift_y + cells_y,
            1 - shift_z : 1 - shift_z + cells_z,
        ]
        nearby = padded[
            19,
            1 - shift_x : 1 - shift_x + cells_x,
            1 - shift_y : 1 - shift_y + cells_y,
            1 - shift_z : 1 - shift_z + cells_z,
        ]
        reverse = resident[opposite_index[component]]
        lattice_weight = weight_table[component]
        projection = project_onto(component, current)
        rebuilt = (
            2.0 * lattice_weight * (1.0 + 4.5 * projection * projection - 1.5 * speed_square)
            - reverse
        )
        read.append(jnp.where(nearby < 0.0, reverse, jnp.where(nearby == 0.0, rebuilt, pulled)))
        weighting = jnp.where(
            nearby >= 1.0, 1.0, jnp.where(nearby > 0.0, 0.5 * (fill_level + nearby), 0.0)
        )
        exchanged = exchanged + weighting * (pulled - reverse)
    liquid = cell_flag <= 1
    exchanged = jnp.where(cell_flag == 1, exchanged, 0.0)
    density = read[0]
    for component in range(1, 19):
        density = density + read[component]
    velocity = momentum(read)
    velocity[2] = velocity[2] - relax_time * gravity
    velocity_square = (
        velocity[0] * velocity[0] + velocity[1] * velocity[1] + velocity[2] * velocity[2]
    )
    relaxed = []
    for component in range(19):
        lattice_weight = weight_table[component]
        if component == 0:
            equilibrium = lattice_weight * (density - 1.5 * velocity_square)
        else:
            projection = project_onto(component, velocity)
            equilibrium = lattice_weight * (
                density + 3.0 * projection + 4.5 * projection * projection - 1.5 * velocity_square
            )
        updated = read[component] - (read[component] - equilibrium) / relax_time
        relaxed.append(jnp.where(liquid, updated, lattice_weight))
    bottom = jnp.where(liquid[:, :, 0], density[:, :, 0] / 3.0, 0.0)
    return (jnp.stack(relaxed), exchanged, bottom)


def per_device(populations, cell_flags, fill_level, tile_block, deck_weights):
    current_pops = populations
    exchanged_total = jnp.zeros(fill_level.shape, jnp.float32)
    bottoms = []
    for step_index in range(cell_flags.shape[0]):
        cell_flag = cell_flags[step_index]
        stacked = jnp.concatenate([current_pops, phase_of(cell_flag, fill_level)[None]], axis=0)
        framed = with_halo(stacked, (("gx", 1), ("gy", 2)), 1)
        relaxed, exchanged, bottom = advance(pad_depth(framed), current_pops, fill_level, cell_flag)
        current_pops = relaxed
        exchanged_total = exchanged_total + exchanged
        bottoms.append(bottom)
    step_count = cell_flags.shape[0]
    tile_count = deck_weights.shape[0]
    block_size = deck_weights.shape[3]
    deck_rows = jnp.stack(bottoms).astype(jnp.bfloat16)
    deck_tiles = deck_rows.reshape(step_count, tile_count, deck_weights.shape[2])
    tile_weights = deck_weights.reshape(tile_count, deck_weights.shape[2], block_size)
    partials = jnp.einsum(
        "stc,tck->tsk", deck_tiles, tile_weights, preferred_element_type=jnp.float32
    )
    partials = partials.reshape(tile_count, step_count * block_size)
    targets = tile_block.reshape(tile_count)
    block_ids = jnp.arange(1 * lax.axis_size(("gx", "gy")), dtype=jnp.int32)
    picker = (block_ids[:, None] == targets[None, :]).astype(jnp.float32)
    summed = jnp.dot(
        picker, partials, precision=lax.Precision.HIGHEST, preferred_element_type=jnp.float32
    )
    shell_loads = lax.psum_scatter(
        summed.reshape(1 * lax.axis_size(("gx", "gy")), step_count, block_size),
        ("gx", "gy"),
        scatter_dimension=0,
        tiled=True,
    )
    return (current_pops, exchanged_total, shell_loads)


def solution(mesh):
    placed = (
        P(None, "gx", "gy", None),
        P(None, "gx", "gy", None),
        P("gx", "gy", None),
        P("gx", "gy"),
        P("gx", "gy", None, None),
    )
    return jax.shard_map(
        per_device,
        mesh=mesh,
        in_specs=placed,
        out_specs=(P(None, "gx", "gy", None), P("gx", "gy", None), P(("gx", "gy"), None, None)),
        check_vma=False,
    )
```

profile of v0, /device:TPU:1, one launch (start us, length us, event | category | flops | bytes accessed | tf_op | source)
XLA Modules:
  0.0 450.2 jit_solution(16526899161957233268)
XLA Ops:
  7.2 1.0 fusion.1877
  8.2 1.0 pad_maximum_fusion.5
  9.3 5.1 %collective-permute-start.1 = (f32[20,1,16,128]{3,2,1,0:T(8,128)S(1)}, f32[20,1,16,128]{3,2,1,0:T(8,128)S(1)}, u32[]{:S(2)}, u32[]{:S(2)}) collective-permute-start(f32[20,1,16,128]{3,2,1,0:T(8,128)S(1)} %get-tuple-element.518), channel_id=1, source_target_pairs={{8,0},{16,8},{24,16},{32,24},{40,32},{48,40},{56,48},{64,56},{72,6... | collective-permute-start | bytes 491528 | tf_op jit(solution)/shard_map/ppermute | solution.py:41
  14.4 3.1 collective-permute-start
  18.3 2.1 collective-permute-done.1
  20.5 1.3 collective-permute-start.3
  21.8 4.9 %collective-permute-start.2 = (f32[20,10,1,128]{3,2,1,0:T(1,128)S(1)}, f32[20,10,1,128]{3,2,1,0:T(1,128)S(1)}, u32[]{:S(2)}, u32[]{:S(2)}) collective-permute-start(f32[20,10,1,128]{3,2,1,0:T(1,128)S(1)} %get-tuple-element.509), channel_id=1, source_target_pairs={{0,1},{1,2},{2,3},{3,4},{4,5},{5,6},{6,7},{8,9},{9,10},{10,11},{11... | collective-permute-start | bytes 307208 | tf_op jit(solution)/shard_map/ppermute | solution.py:38
  26.8 0.9 collective-permute-done.3
  28.5 7.6 %pad_maximum_fusion.3 = (f32[20,10,18,129]{3,2,1,0:T(8,128)S(1)}, f32[20,10,18,129]{3,2,1,0:T(8,128)}) fusion(f32[20,10,18,1]{3,2,1,0:T(8,128)} %constant.222.clone.1, f32[20,10,1,128]{3,2,1,0:T(1,128)S(1)} %collective-permute-done.3, f32[20,1,16,128]{3,2,1,0:T(8,128)S(1)} %collective-permute-done.1, f32[1,8,16,128]{3,2,1,0:T(8,128)S(1)} %get-tuple-element.479, ...), kind=kLoop, calls=%fused_computation.3 | loop fusion | flops 8359200 | bytes 5572800 | tf_op jit(solution)/shard_map/concatenate | solution.py:81
  36.1 4.1 fusion.1760
  40.3 2.5 constant_dynamic-update-slice_fusion.19
  44.4 1.9 collective-permute-start.5
  46.4 7.0 %collective-permute-start.4 = (f32[20,1,16,128]{3,2,1,0:T(8,128)S(1)}, f32[20,1,16,128]{3,2,1,0:T(8,128)S(1)}, u32[]{:S(2)}, u32[]{:S(2)}) collective-permute-start(f32[20,1,16,128]{3,2,1,0:T(8,128)S(1)} %get-tuple-element.515), channel_id=1, source_target_pairs={{0,8},{8,16},{16,24},{24,32},{32,40},{40,48},{48,56},{56,64},{64,7... | collective-permute-start | bytes 491528 | tf_op jit(solution)/shard_map/ppermute | solution.py:38
  54.5 1.2 collective-permute-done.4
  55.8 1.3 collective-permute-start.7
  57.1 5.5 %collective-permute-start.6 = (f32[20,10,1,128]{3,2,1,0:T(1,128)S(1)}, f32[20,10,1,128]{3,2,1,0:T(1,128)S(1)}, u32[]{:S(2)}, u32[]{:S(2)}) collective-permute-start(f32[20,10,1,128]{3,2,1,0:T(1,128)S(1)} %get-tuple-element.507), channel_id=1, source_target_pairs={{0,1},{1,2},{2,3},{3,4},{4,5},{5,6},{6,7},{8,9},{9,10},{10,11},{11... | collective-permute-start | bytes 307208 | tf_op jit(solution)/shard_map/ppermute | solution.py:38
  62.7 1.5 collective-permute-done.6
  64.3 3.9 pad_maximum_fusion.2
  68.4 2.2 subtract_select_fusion.3
  73.1 1.9 collective-permute-start.9
  75.1 6.2 %collective-permute-start.8 = (f32[20,1,16,128]{3,2,1,0:T(8,128)S(1)}, f32[20,1,16,128]{3,2,1,0:T(8,128)S(1)}, u32[]{:S(2)}, u32[]{:S(2)}) collective-permute-start(f32[20,1,16,128]{3,2,1,0:T(8,128)S(1)} %get-tuple-element.513), channel_id=1, source_target_pairs={{0,8},{8,16},{16,24},{24,32},{32,40},{40,48},{48,56},{56,64},{64,7... | collective-permute-start | bytes 491528 | tf_op jit(solution)/shard_map/ppermute | solution.py:38
  82.4 1.2 collective-permute-done.8
  83.7 1.3 collective-permute-start.11
  85.0 5.7 %collective-permute-start.10 = (f32[20,10,1,128]{3,2,1,0:T(1,128)S(1)}, f32[20,10,1,128]{3,2,1,0:T(1,128)S(1)}, u32[]{:S(2)}, u32[]{:S(2)}) collective-permute-start(f32[20,10,1,128]{3,2,1,0:T(1,128)S(1)} %get-tuple-element.505), channel_id=1, source_target_pairs={{0,1},{1,2},{2,3},{3,4},{4,5},{5,6},{6,7},{8,9},{9,10},{10,11},{11... | collective-permute-start | bytes 307208 | tf_op jit(solution)/shard_map/ppermute | solution.py:38
  91.1 1.0 collective-permute-done.10
  92.1 3.9 pad_maximum_fusion.1
  96.3 2.4 add_multiply_fusion.1
  98.8 1.7 constant_dynamic-update-slice_fusion.59
  113.2 0.8 fusion.2109
  114.0 1.9 collective-permute-start.13
  115.9 6.1 %collective-permute-start.12 = (f32[20,1,16,128]{3,2,1,0:T(8,128)}, f32[20,1,16,128]{3,2,1,0:T(8,128)S(1)}, u32[]{:S(2)}, u32[]{:S(2)}) collective-permute-start(f32[20,1,16,128]{3,2,1,0:T(8,128)} %get-tuple-element.511), channel_id=1, source_target_pairs={{0,8},{8,16},{16,24},{24,32},{32,40},{40,48},{48,56},{56,64},{64,7... | collective-permute-start | bytes 491528 | tf_op jit(solution)/shard_map/ppermute | solution.py:38
  122.8 1.3 select_n.11291
  124.1 1.5 fusion.1887
  125.6 1.3 select_n.11292
  127.1 1.4 collective-permute-start.15
  128.6 5.4 %collective-permute-start.14 = (f32[20,10,1,128]{3,2,1,0:T(1,128)S(1)}, f32[20,10,1,128]{3,2,1,0:T(1,128)S(1)}, u32[]{:S(2)}, u32[]{:S(2)}) collective-permute-start(f32[20,10,1,128]{3,2,1,0:T(1,128)S(1)} %get-tuple-element.503), channel_id=1, source_target_pairs={{0,1},{1,2},{2,3},{3,4},{4,5},{5,6},{6,7},{8,9},{9,10},{10,11},{11... | collective-permute-start | bytes 307208 | tf_op jit(solution)/shard_map/ppermute | solution.py:38
  134.0 1.4 add_multiply_fusion.8
  135.6 5.1 %pad_maximum_fusion = (f32[20,10,18,129]{3,2,1,0:T(8,128)S(1)}, f32[20,10,18,129]{3,2,1,0:T(8,128)}) fusion(f32[20,10,18,1]{3,2,1,0:T(8,128)S(1)} %copy-done.3, f32[20,10,1,128]{3,2,1,0:T(1,128)S(1)} %collective-permute-done.15, f32[20,1,16,128]{3,2,1,0:T(8,128)S(1)} %collective-permute-done.13, f32[20,8,16,128]{3,2,1,0:T(8,128)S(1)} %get-tuple-element.277, ...), kind=kLoop, calls=%fused_computation | loop fusion | flops 6966000 | bytes 5572800 | tf_op jit(solution)/shard_map/concatenate | solution.py:81
  140.7 2.0 slice_bitcast_fusion.5
  143.1 3.4 fusion.1390
  146.7 1.5 fusion.1444
  148.4 3.0 constant_dynamic-update-slice_fusion.78
  152.8 1.9 fusion.1890
  154.7 4.7 %copy.22 = f32[256,4,1024]{2,1,0:T(4,128)} copy(f32[256,4,1024]{2,0,1:T(8,128)S(1)} %fusion.1890) | data formatting | bytes 8388608 | tf_op jit(solution)/shard_map/dot_general | solution.py:167
  167.7 1.7 constant_dynamic-update-slice_fusion.65
  173.2 12.7 %fusion.1487 = f32[8,16,128]{2,1,0:T(8,128)} fusion(f32[8,16,128]{2,1,0:T(8,128)S(1)} %copy-done.15, f32[8,16,128]{2,1,0:T(8,128)S(1)} %copy-done.10, f32[8,16,128]{2,1,0:T(8,128)} %copy-done.157, f32[8,16,128]{2,1,0:T(8,128)} %get-tuple-element.64, f32[8,16,128]{2,1,0:T(8,128)} %get-tuple-element.63, f32[8,16,128]{2,1,0:T(8,128)} %get-tuple-element.62, ...), kind=kLoop, calls=%fused_computation.1925 | loop fusion | flops 10665984 | bytes 14352384 | tf_op jit(solution)/shard_map/add | solution.py:152
  185.9 256.1 %all-reduce.7.cloned.1.call-done = f32[256,4,1024]{2,1,0:T(4,128)} async-done(((f32[256,4,1024]{2,1,0:T(4,128)}), f32[256,4,1024]{2,1,0:T(4,128)}) %all-reduce.7.cloned.1.call-update) | async-done | bytes 4194320
  442.0 1.3 constant_dynamic-slice_fusion
  (514 shorter events, 34.7 us)
Async XLA Ops:
  7.2 145.4 %copy-start = (bf16[2,1,64,1024]{3,2,1,0:T(8,128)(2,1)S(1)}, bf16[2,1,64,1024]{3,2,1,0:T(8,128)(2,1)}, u32[]{:S(2)}) copy-start(bf16[2,1,64,1024]{3,2,1,0:T(8,128)(2,1)} %param.17) | copy-start | bytes 786436
  7.2 434.8 %all-reduce.7.cloned.1.call-start = ((), (), s32[]{:S(2)}) async-start(), calls=%async_computation | async-start | bytes 8388608
  9.3 11.0 %collective-permute-start.1 = (f32[20,1,16,128]{3,2,1,0:T(8,128)S(1)}, f32[20,1,16,128]{3,2,1,0:T(8,128)S(1)}, u32[]{:S(2)}, u32[]{:S(2)}) collective-permute-start(f32[20,1,16,128]{3,2,1,0:T(8,128)S(1)} %get-tuple-element.518), channel_id=1, source_target_pairs={{8,0},{16,8},{24,16},{32,24},{40,32},{48,40},{56,48},{64,56},{72,6... | collective-permute-start | bytes 491528 | tf_op jit(solution)/shard_map/ppermute | solution.py:41
  14.4 5.9 %collective-permute-start = (f32[20,1,16,128]{3,2,1,0:T(8,128)S(1)}, f32[20,1,16,128]{3,2,1,0:T(8,128)S(1)}, u32[]{:S(2)}, u32[]{:S(2)}) collective-permute-start(f32[20,1,16,128]{3,2,1,0:T(8,128)S(1)} %get-tuple-element.517), channel_id=1, source_target_pairs={{0,8},{8,16},{16,24},{24,32},{32,40},{40,48},{48,56},{56,64},{64,7... | collective-permute-start | bytes 491528 | tf_op jit(solution)/shard_map/ppermute | solution.py:38
  20.5 7.3 %collective-permute-start.3 = (f32[20,10,1,128]{3,2,1,0:T(1,128)S(1)}, f32[20,10,1,128]{3,2,1,0:T(1,128)S(1)}, u32[]{:S(2)}, u32[]{:S(2)}) collective-permute-start(f32[20,10,1,128]{3,2,1,0:T(1,128)S(1)} %get-tuple-element.510), channel_id=1, source_target_pairs={{1,0},{2,1},{3,2},{4,3},{5,4},{6,5},{7,6},{9,8},{10,9},{11,10},{12... | collective-permute-start | bytes 307208 | tf_op jit(solution)/shard_map/ppermute | solution.py:41
  21.8 6.7 %collective-permute-start.2 = (f32[20,10,1,128]{3,2,1,0:T(1,128)S(1)}, f32[20,10,1,128]{3,2,1,0:T(1,128)S(1)}, u32[]{:S(2)}, u32[]{:S(2)}) collective-permute-start(f32[20,10,1,128]{3,2,1,0:T(1,128)S(1)} %get-tuple-element.509), channel_id=1, source_target_pairs={{0,1},{1,2},{2,3},{3,4},{4,5},{5,6},{6,7},{8,9},{9,10},{10,11},{11... | collective-permute-start | bytes 307208 | tf_op jit(solution)/shard_map/ppermute | solution.py:38
  44.4 10.0 %collective-permute-start.5 = (f32[20,1,16,128]{3,2,1,0:T(8,128)S(1)}, f32[20,1,16,128]{3,2,1,0:T(8,128)S(1)}, u32[]{:S(2)}, u32[]{:S(2)}) collective-permute-start(f32[20,1,16,128]{3,2,1,0:T(8,128)S(1)} %get-tuple-element.516), channel_id=1, source_target_pairs={{8,0},{16,8},{24,16},{32,24},{40,32},{48,40},{56,48},{64,56},{72,6... | collective-permute-start | bytes 491528 | tf_op jit(solution)/shard_map/ppermute | solution.py:41
  46.4 9.3 %collective-permute-start.4 = (f32[20,1,16,128]{3,2,1,0:T(8,128)S(1)}, f32[20,1,16,128]{3,2,1,0:T(8,128)S(1)}, u32[]{:S(2)}, u32[]{:S(2)}) collective-permute-start(f32[20,1,16,128]{3,2,1,0:T(8,128)S(1)} %get-tuple-element.515), channel_id=1, source_target_pairs={{0,8},{8,16},{16,24},{24,32},{32,40},{40,48},{48,56},{56,64},{64,7... | collective-permute-start | bytes 491528 | tf_op jit(solution)/shard_map/ppermute | solution.py:38
  54.0 14.2 %copy-start.118 = (f32[8,16,128]{2,1,0:T(8,128)}, f32[8,16,128]{2,1,0:T(8,128)S(1)}, u32[]{:S(2)}) copy-start(f32[8,16,128]{2,1,0:T(8,128)S(1)} %get-tuple-element.228) | copy-start | bytes 196612
  54.0 14.2 %copy-start.119 = (f32[8,16,128]{2,1,0:T(8,128)}, f32[8,16,128]{2,1,0:T(8,128)S(1)}, u32[]{:S(2)}) copy-start(f32[8,16,128]{2,1,0:T(8,128)S(1)} %get-tuple-element.229) | copy-start | bytes 196612
  54.0 14.2 %copy-start.120 = (f32[8,16,128]{2,1,0:T(8,128)}, f32[8,16,128]{2,1,0:T(8,128)S(1)}, u32[]{:S(2)}) copy-start(f32[8,16,128]{2,1,0:T(8,128)S(1)} %get-tuple-element.231) | copy-start | bytes 196612
  54.0 14.2 %copy-start.121 = (f32[8,16,128]{2,1,0:T(8,128)}, f32[8,16,128]{2,1,0:T(8,128)S(1)}, u32[]{:S(2)}) copy-start(f32[8,16,128]{2,1,0:T(8,128)S(1)} %get-tuple-element.232) | copy-start | bytes 196612
  54.1 14.2 %copy-start.122 = (f32[8,16,128]{2,1,0:T(8,128)}, f32[8,16,128]{2,1,0:T(8,128)S(1)}, u32[]{:S(2)}) copy-start(f32[8,16,128]{2,1,0:T(8,128)S(1)} %get-tuple-element.233) | copy-start | bytes 196612
  54.1 14.2 %copy-start.123 = (f32[8,16,128]{2,1,0:T(8,128)}, f32[8,16,128]{2,1,0:T(8,128)S(1)}, u32[]{:S(2)}) copy-start(f32[8,16,128]{2,1,0:T(8,128)S(1)} %get-tuple-element.234) | copy-start | bytes 196612
  54.1 14.2 %copy-start.124 = (f32[8,16,128]{2,1,0:T(8,128)}, f32[8,16,128]{2,1,0:T(8,128)S(1)}, u32[]{:S(2)}) copy-start(f32[8,16,128]{2,1,0:T(8,128)S(1)} %get-tuple-element.235) | copy-start | bytes 196612
  54.1 14.2 %copy-start.125 = (f32[8,16,128]{2,1,0:T(8,128)}, f32[8,16,128]{2,1,0:T(8,128)S(1)}, u32[]{:S(2)}) copy-start(f32[8,16,128]{2,1,0:T(8,128)S(1)} %get-tuple-element.236) | copy-start | bytes 196612
  54.1 14.2 %copy-start.126 = (f32[8,16,128]{2,1,0:T(8,128)}, f32[8,16,128]{2,1,0:T(8,128)S(1)}, u32[]{:S(2)}) copy-start(f32[8,16,128]{2,1,0:T(8,128)S(1)} %get-tuple-element.238) | copy-start | bytes 196612
  54.1 14.2 %copy-start.127 = (f32[8,16,128]{2,1,0:T(8,128)}, f32[8,16,128]{2,1,0:T(8,128)S(1)}, u32[]{:S(2)}) copy-start(f32[8,16,128]{2,1,0:T(8,128)S(1)} %get-tuple-element.239) | copy-start | bytes 196612
  54.1 14.2 %copy-start.128 = (f32[8,16,128]{2,1,0:T(8,128)}, f32[8,16,128]{2,1,0:T(8,128)S(1)}, u32[]{:S(2)}) copy-start(f32[8,16,128]{2,1,0:T(8,128)S(1)} %get-tuple-element.240) | copy-start | bytes 196612
  54.1 14.2 %copy-start.129 = (f32[8,16,128]{2,1,0:T(8,128)}, f32[8,16,128]{2,1,0:T(8,128)S(1)}, u32[]{:S(2)}) copy-start(f32[8,16,128]{2,1,0:T(8,128)S(1)} %get-tuple-element.241) | copy-start | bytes 196612
  54.1 14.2 %copy-start.130 = (f32[8,16,128]{2,1,0:T(8,128)}, f32[8,16,128]{2,1,0:T(8,128)S(1)}, u32[]{:S(2)}) copy-start(f32[8,16,128]{2,1,0:T(8,128)S(1)} %get-tuple-element.242) | copy-start | bytes 196612
  54.1 14.2 %copy-start.131 = (f32[8,16,128]{2,1,0:T(8,128)}, f32[8,16,128]{2,1,0:T(8,128)S(1)}, u32[]{:S(2)}) copy-start(f32[8,16,128]{2,1,0:T(8,128)S(1)} %get-tuple-element.243) | copy-start | bytes 196612
  54.2 14.2 %copy-start.132 = (f32[8,16,128]{2,1,0:T(8,128)}, f32[8,16,128]{2,1,0:T(8,128)S(1)}, u32[]{:S(2)}) copy-start(f32[8,16,128]{2,1,0:T(8,128)S(1)} %get-tuple-element.244) | copy-start | bytes 196612
  54.2 14.2 %copy-start.133 = (f32[8,16,128]{2,1,0:T(8,128)}, f32[8,16,128]{2,1,0:T(8,128)S(1)}, u32[]{:S(2)}) copy-start(f32[8,16,128]{2,1,0:T(8,128)S(1)} %get-tuple-element.245) | copy-start | bytes 196612
  54.2 14.2 %copy-start.134 = (f32[8,16,128]{2,1,0:T(8,128)}, f32[8,16,128]{2,1,0:T(8,128)S(1)}, u32[]{:S(2)}) copy-start(f32[8,16,128]{2,1,0:T(8,128)S(1)} %get-tuple-element.246) | copy-start | bytes 196612
  54.2 14.2 %copy-start.135 = (f32[8,16,128]{2,1,0:T(8,128)}, f32[8,16,128]{2,1,0:T(8,128)S(1)}, u32[]{:S(2)}) copy-start(f32[8,16,128]{2,1,0:T(8,128)S(1)} %get-tuple-element.247) | copy-start | bytes 196612
  55.8 6.9 %collective-permute-start.7 = (f32[20,10,1,128]{3,2,1,0:T(1,128)S(1)}, f32[20,10,1,128]{3,2,1,0:T(1,128)S(1)}, u32[]{:S(2)}, u32[]{:S(2)}) collective-permute-start(f32[20,10,1,128]{3,2,1,0:T(1,128)S(1)} %get-tuple-element.508), channel_id=1, source_target_pairs={{1,0},{2,1},{3,2},{4,3},{5,4},{6,5},{7,6},{9,8},{10,9},{11,10},{12... | collective-permute-start | bytes 307208 | tf_op jit(solution)/shard_map/ppermute | solution.py:41
  57.1 7.2 %collective-permute-start.6 = (f32[20,10,1,128]{3,2,1,0:T(1,128)S(1)}, f32[20,10,1,128]{3,2,1,0:T(1,128)S(1)}, u32[]{:S(2)}, u32[]{:S(2)}) collective-permute-start(f32[20,10,1,128]{3,2,1,0:T(1,128)S(1)} %get-tuple-element.507), channel_id=1, source_target_pairs={{0,1},{1,2},{2,3},{3,4},{4,5},{5,6},{6,7},{8,9},{9,10},{10,11},{11... | collective-permute-start | bytes 307208 | tf_op jit(solution)/shard_map/ppermute | solution.py:38
  73.1 9.2 %collective-permute-start.9 = (f32[20,1,16,128]{3,2,1,0:T(8,128)S(1)}, f32[20,1,16,128]{3,2,1,0:T(8,128)S(1)}, u32[]{:S(2)}, u32[]{:S(2)}) collective-permute-start(f32[20,1,16,128]{3,2,1,0:T(8,128)S(1)} %get-tuple-element.514), channel_id=1, source_target_pairs={{8,0},{16,8},{24,16},{32,24},{40,32},{48,40},{56,48},{64,56},{72,6... | collective-permute-start | bytes 491528 | tf_op jit(solution)/shard_map/ppermute | solution.py:41
  75.1 8.5 %collective-permute-start.8 = (f32[20,1,16,128]{3,2,1,0:T(8,128)S(1)}, f32[20,1,16,128]{3,2,1,0:T(8,128)S(1)}, u32[]{:S(2)}, u32[]{:S(2)}) collective-permute-start(f32[20,1,16,128]{3,2,1,0:T(8,128)S(1)} %get-tuple-element.513), channel_id=1, source_target_pairs={{0,8},{8,16},{16,24},{24,32},{32,40},{40,48},{48,56},{56,64},{64,7... | collective-permute-start | bytes 491528 | tf_op jit(solution)/shard_map/ppermute | solution.py:38
  81.9 14.2 %copy-start.136 = (f32[8,16,128]{2,1,0:T(8,128)}, f32[8,16,128]{2,1,0:T(8,128)S(1)}, u32[]{:S(2)}) copy-start(f32[8,16,128]{2,1,0:T(8,128)S(1)} %get-tuple-element.165) | copy-start | bytes 196612
  81.9 14.2 %copy-start.137 = (f32[8,16,128]{2,1,0:T(8,128)}, f32[8,16,128]{2,1,0:T(8,128)S(1)}, u32[]{:S(2)}) copy-start(f32[8,16,128]{2,1,0:T(8,128)S(1)} %get-tuple-element.166) | copy-start | bytes 196612
  81.9 14.2 %copy-start.138 = (f32[8,16,128]{2,1,0:T(8,128)}, f32[8,16,128]{2,1,0:T(8,128)S(1)}, u32[]{:S(2)}) copy-start(f32[8,16,128]{2,1,0:T(8,128)S(1)} %get-tuple-element.168) | copy-start | bytes 196612
  81.9 14.2 %copy-start.139 = (f32[8,16,128]{2,1,0:T(8,128)}, f32[8,16,128]{2,1,0:T(8,128)S(1)}, u32[]{:S(2)}) copy-start(f32[8,16,128]{2,1,0:T(8,128)S(1)} %get-tuple-element.169) | copy-start | bytes 196612
  81.9 14.2 %copy-start.140 = (f32[8,16,128]{2,1,0:T(8,128)}, f32[8,16,128]{2,1,0:T(8,128)S(1)}, u32[]{:S(2)}) copy-start(f32[8,16,128]{2,1,0:T(8,128)S(1)} %get-tuple-element.170) | copy-start | bytes 196612
  82.0 14.2 %copy-start.141 = (f32[8,16,128]{2,1,0:T(8,128)}, f32[8,16,128]{2,1,0:T(8,128)S(1)}, u32[]{:S(2)}) copy-start(f32[8,16,128]{2,1,0:T(8,128)S(1)} %get-tuple-element.171) | copy-start | bytes 196612
  82.0 14.2 %copy-start.142 = (f32[8,16,128]{2,1,0:T(8,128)}, f32[8,16,128]{2,1,0:T(8,128)S(1)}, u32[]{:S(2)}) copy-start(f32[8,16,128]{2,1,0:T(8,128)S(1)} %get-tuple-element.172) | copy-start | bytes 196612
  82.0 14.2 %copy-start.143 = (f32[8,16,128]{2,1,0:T(8,128)}, f32[8,16,128]{2,1,0:T(8,128)S(1)}, u32[]{:S(2)}) copy-start(f32[8,16,128]{2,1,0:T(8,128)S(1)} %get-tuple-element.173) | copy-start | bytes 196612
  82.0 14.2 %copy-start.144 = (f32[8,16,128]{2,1,0:T(8,128)}, f32[8,16,128]{2,1,0:T(8,128)S(1)}, u32[]{:S(2)}) copy-start(f32[8,16,128]{2,1,0:T(8,128)S(1)} %get-tuple-element.175) | copy-start | bytes 196612
  82.0 14.2 %copy-start.145 = (f32[8,16,128]{2,1,0:T(8,128)}, f32[8,16,128]{2,1,0:T(8,128)S(1)}, u32[]{:S(2)}) copy-start(f32[8,16,128]{2,1,0:T(8,128)S(1)} %get-tuple-element.176) | copy-start | bytes 196612
  82.0 14.2 %copy-start.146 = (f32[8,16,128]{2,1,0:T(8,128)}, f32[8,16,128]{2,1,0:T(8,128)S(1)}, u32[]{:S(2)}) copy-start(f32[8,16,128]{2,1,0:T(8,128)S(1)} %get-tuple-element.177) | copy-start | bytes 196612
  82.0 14.2 %copy-start.147 = (f32[8,16,128]{2,1,0:T(8,128)}, f32[8,16,128]{2,1,0:T(8,128)S(1)}, u32[]{:S(2)}) copy-start(f32[8,16,128]{2,1,0:T(8,128)S(1)} %get-tuple-element.178) | copy-start | bytes 196612
  83.7 7.5 %collective-permute-start.11 = (f32[20,10,1,128]{3,2,1,0:T(1,128)S(1)}, f32[20,10,1,128]{3,2,1,0:T(1,128)S(1)}, u32[]{:S(2)}, u32[]{:S(2)}) collective-permute-start(f32[20,10,1,128]{3,2,1,0:T(1,128)S(1)} %get-tuple-element.506), channel_id=1, source_target_pairs={{1,0},{2,1},{3,2},{4,3},{5,4},{6,5},{7,6},{9,8},{10,9},{11,10},{12... | collective-permute-start | bytes 307208 | tf_op jit(solution)/shard_map/ppermute | solution.py:41
  85.0 7.1 %collective-permute-start.10 = (f32[20,10,1,128]{3,2,1,0:T(1,128)S(1)}, f32[20,10,1,128]{3,2,1,0:T(1,128)S(1)}, u32[]{:S(2)}, u32[]{:S(2)}) collective-permute-start(f32[20,10,1,128]{3,2,1,0:T(1,128)S(1)} %get-tuple-element.505), channel_id=1, source_target_pairs={{0,1},{1,2},{2,3},{3,4},{4,5},{5,6},{6,7},{8,9},{9,10},{10,11},{11... | collective-permute-start | bytes 307208 | tf_op jit(solution)/shard_map/ppermute | solution.py:38
  114.0 13.0 %collective-permute-start.13 = (f32[20,1,16,128]{3,2,1,0:T(8,128)}, f32[20,1,16,128]{3,2,1,0:T(8,128)S(1)}, u32[]{:S(2)}, u32[]{:S(2)}) collective-permute-start(f32[20,1,16,128]{3,2,1,0:T(8,128)} %get-tuple-element.512), channel_id=1, source_target_pairs={{8,0},{16,8},{24,16},{32,24},{40,32},{48,40},{56,48},{64,56},{72,6... | collective-permute-start | bytes 491528 | tf_op jit(solution)/shard_map/ppermute | solution.py:41
  115.9 11.0 %collective-permute-start.12 = (f32[20,1,16,128]{3,2,1,0:T(8,128)}, f32[20,1,16,128]{3,2,1,0:T(8,128)S(1)}, u32[]{:S(2)}, u32[]{:S(2)}) collective-permute-start(f32[20,1,16,128]{3,2,1,0:T(8,128)} %get-tuple-element.511), channel_id=1, source_target_pairs={{0,8},{8,16},{16,24},{24,32},{32,40},{40,48},{48,56},{56,64},{64,7... | collective-permute-start | bytes 491528 | tf_op jit(solution)/shard_map/ppermute | solution.py:38
  127.1 8.4 %collective-permute-start.15 = (f32[20,10,1,128]{3,2,1,0:T(1,128)S(1)}, f32[20,10,1,128]{3,2,1,0:T(1,128)S(1)}, u32[]{:S(2)}, u32[]{:S(2)}) collective-permute-start(f32[20,10,1,128]{3,2,1,0:T(1,128)S(1)} %get-tuple-element.504), channel_id=1, source_target_pairs={{1,0},{2,1},{3,2},{4,3},{5,4},{6,5},{7,6},{9,8},{10,9},{11,10},{12... | collective-permute-start | bytes 307208 | tf_op jit(solution)/shard_map/ppermute | solution.py:41
  128.6 7.1 %collective-permute-start.14 = (f32[20,10,1,128]{3,2,1,0:T(1,128)S(1)}, f32[20,10,1,128]{3,2,1,0:T(1,128)S(1)}, u32[]{:S(2)}, u32[]{:S(2)}) collective-permute-start(f32[20,10,1,128]{3,2,1,0:T(1,128)S(1)} %get-tuple-element.503), channel_id=1, source_target_pairs={{0,1},{1,2},{2,3},{3,4},{4,5},{5,6},{6,7},{8,9},{9,10},{10,11},{11... | collective-permute-start | bytes 307208 | tf_op jit(solution)/shard_map/ppermute | solution.py:38
  (173 other events, 856.7 us)
Sparse Core Ops, SparseCore 0:
  159.5 282.4 all-reduce.6
where the time goes:
time: 452 us; the launch traced here: 450 us
  waiting for transfers between devices  266 us (59%)
  other arithmetic  90.6 us (20%)
  starting transfers between devices  60.1 us (13%)
  between operations  17.4 us (4%)
  local copies, waits for them, and re-layouts  14.3 us (3%)
    unnamed x2, waiting for transfers between devices  256 us
    ppermute x8, starting transfers between devices, with_halo(): lax.ppermute(lax.slice_in_dim(block, block.shape[dim] - width, None, axis...  43.9 us
    unnamed x75, other arithmetic  33.7 us
    concatenate x4, other arithmetic, pad_depth(): return jnp.concatenate([below, block, above], axis=3)  20.5 us
    ppermute x8, starting transfers between devices, with_halo(): lax.ppermute(lax.slice_in_dim(block, 0, width, axis=dim), axis, backward)  16.2 us
    add x1, other arithmetic, per_device(): exchanged_total = exchanged_total + exchanged  12.7 us
  transfers between devices with their start and end apart: 17, of which 11 were waited for; matrix products, arithmetic and copies ran while one was open for 8% of the time, Pallas kernels for 0%

commit v1 on v0

v1 whole, which is shorter than its diff:
```python
import functools

import jax
import jax.numpy as jnp
from jax import lax
from jax.experimental import pallas as pl
from jax.experimental.pallas import tpu as pltpu
from jax.sharding import PartitionSpec as P

velocity_table = (
    (0, 0, 0),
    (1, 0, 0),
    (-1, 0, 0),
    (0, 1, 0),
    (0, -1, 0),
    (0, 0, 1),
    (0, 0, -1),
    (1, 1, 0),
    (-1, -1, 0),
    (1, -1, 0),
    (-1, 1, 0),
    (1, 0, 1),
    (-1, 0, -1),
    (1, 0, -1),
    (-1, 0, 1),
    (0, 1, 1),
    (0, -1, -1),
    (0, 1, -1),
    (0, -1, 1),
)
weight_table = (1.0 / 3.0,) + (1.0 / 18.0,) * 6 + (1.0 / 36.0,) * 12
relax_time = 0.8
gravity = 0.001

MESH = pl.DeviceIdType.MESH
F32 = jnp.float32
STEPS = 4
CX, CY, NZ = 8, 16, 128
CELLS = CX * CY
PITCH = 24
ROWS = 248
LOW_SLAB = 8
HIGH_SLAB = PITCH * (CX + 1) + 8
X_PLUS = (1, 7, 9, 11, 13)
X_MINUS = (2, 8, 10, 12, 14)
Y_PLUS = (3, 7, 10, 15, 17)
Y_MINUS = (4, 8, 9, 16, 18)
SLOTS = X_PLUS + X_MINUS + (3, 4, 5, 6, 15, 16, 17, 18)
SLOT = {component: place for place, component in enumerate(SLOTS)}
FLUID, GAS, WALL = 1.0, -0.5, -1.0


def row_of(x, y):
    return PITCH * (x + 1) + 8 + y


def turned(block, shift):
    if shift == 0:
        return block
    return pltpu.roll(block, shift % NZ, block.ndim - 1)


def version_of(shift_z):
    return 0 if shift_z == 0 else (1 if shift_z == 1 else 2)


def dot3(direction, vector):
    result = None
    for factor, part in zip(direction, vector):
        if factor == 0:
            continue
        if result is None:
            result = part if factor > 0 else -part
        else:
            result = result + part if factor > 0 else result - part
    return result


def add_momentum(totals, direction, difference):
    for axis, factor in enumerate(direction):
        if factor == 0:
            continue
        if totals[axis] is None:
            totals[axis] = difference if factor > 0 else -difference
        elif factor > 0:
            totals[axis] = totals[axis] + difference
        else:
            totals[axis] = totals[axis] - difference


def kernel(
    gx_count,
    gy_count,
    pops_in,
    flags_in,
    fill_in,
    tile_in,
    weights_in,
    pops_out,
    mass_out,
    loads_out,
    streamed,
    resident,
    phases,
    current,
    mass,
    deck,
    flags,
    fill,
    weights_packed,
    weights,
    y_send,
    y_recv,
    corner_recv,
    hy_send,
    hy_recv,
    hcorner_recv,
    tile_send,
    tile_recv,
    index_block,
    index_scalars,
    first0,
    first1,
    first2,
    first3,
    second_send,
    second_recv,
    loads,
    local_sem,
    halo_send_sem,
    halo_recv_sem,
    route_send_sem,
    route_recv_sem,
):
    first = (first0, first1, first2, first3)
    gx = lax.axis_index("gx")
    gy = lax.axis_index("gy")
    group_count = gx_count // 2
    member_count = 2 * gy_count
    group = gx // 2
    member = lax.rem(gx, 2) * gy_count + gy
    east = lax.rem(gx + 1, gx_count)
    west = lax.rem(gx + gx_count - 1, gx_count)
    north = lax.rem(gy + 1, gy_count)
    south = lax.rem(gy + gy_count - 1, gy_count)

    def member_device(shift):
        other = lax.rem(member + shift, member_count)
        return other, (2 * group + other // gy_count, lax.rem(other, gy_count))

    def group_device(shift):
        other = lax.rem(group + shift, group_count)
        return other, (2 * other + lax.rem(gx, 2), gy)

    neighbours = (
        (east, gy),
        (west, gy),
        (gx, north),
        (gx, south),
        (east, north),
        (west, south),
        (east, south),
        (west, north),
    )

    loads_of = [
        pltpu.make_async_copy(flags_in, flags, local_sem.at[0]),
        pltpu.make_async_copy(fill_in, fill, local_sem.at[1]),
        pltpu.make_async_copy(pops_in, resident.at[0], local_sem.at[2]),
        pltpu.make_async_copy(weights_in, weights_packed, local_sem.at[3]),
    ]
    for copy in loads_of:
        copy.start()

    barrier = pltpu.get_barrier_semaphore()
    for device in neighbours:
        pl.semaphore_signal(barrier, inc=1, device_id=device, device_id_type=MESH)
    for shift in range(1, member_count):
        pl.semaphore_signal(
            barrier, inc=1, device_id=member_device(shift)[1], device_id_type=MESH
        )
    for shift in range(1, group_count):
        pl.semaphore_signal(
            barrier, inc=1, device_id=group_device(shift)[1], device_id_type=MESH
        )

    lane = lax.broadcasted_iota(jnp.int32, (8, NZ), 1)

    def put_phase(step, rows, code):
        phases[step, 0, rows, :] = code
        phases[step, 1, rows, :] = jnp.where(lane == 0, WALL, turned(code, 1))
        phases[step, 2, rows, :] = jnp.where(lane == NZ - 1, GAS, turned(code, -1))

    loads_of[0].wait()
    loads_of[1].wait()

    def code_rows(index, carry):
        x = index // 2
        half = lax.rem(index, 2)
        cells = pl.ds(pl.multiple_of(8 * index, 8), 8)
        rows = pl.ds(pl.multiple_of(PITCH * x + 32 + 8 * half, 8), 8)
        level = 0.5 * fill[cells, :]
        for step in range(STEPS):
            kind = flags[step, cells, :]
            code = jnp.where(
                kind == 0, FLUID, jnp.where(kind == 1, level, jnp.where(kind == 2, GAS, WALL))
            )
            put_phase(step, rows, code)
        return carry

    lax.fori_loop(0, 2 * CX, code_rows, 0)
    for step in range(STEPS):
        hy_send[0, step] = phases[step, 0, pl.ds(row_of(0, CY - 1), CX, stride=PITCH), :]
        hy_send[1, step] = phases[step, 0, pl.ds(row_of(0, 0), CX, stride=PITCH), :]

    loads_of[2].wait()

    def first_rows(index, carry):
        x = index // 2
        half = lax.rem(index, 2)
        cells = pl.ds(pl.multiple_of(8 * index, 8), 8)
        rows = pl.ds(pl.multiple_of(PITCH * x + 32 + 8 * half, 8), 8)
        totals = [None, None, None]
        for component in range(1, 19, 2):
            direction = velocity_table[component]
            along = resident[0, component, cells, :]
            against = resident[0, component + 1, cells, :]
            add_momentum(totals, direction, along - against)
            streamed[0, SLOT[component], rows, :] = turned(along, direction[2])
            streamed[0, SLOT[component + 1], rows, :] = turned(against, -direction[2])
        for axis in range(3):
            current[0, axis, cells, :] = totals[axis]
        return carry

    lax.fori_loop(0, 2 * CX, first_rows, 0)
    for side, (y, components) in enumerate(((CY - 1, Y_PLUS), (0, Y_MINUS))):
        for place, component in enumerate(components):
            y_send[0, side, place] = turned(
                resident[0, component, pl.ds(y, CX, stride=CY), :], velocity_table[component][2]
            )

    pl.semaphore_wait(barrier, 8 + member_count - 1 + group_count - 1)

    def remote(source, target, exchange, place, device):
        return pltpu.make_async_remote_copy(
            src_ref=source,
            dst_ref=target,
            send_sem=halo_send_sem.at[exchange, place],
            recv_sem=halo_recv_sem.at[exchange, place],
            device_id=device,
            device_id_type=MESH,
        )

    def y_copies(step):
        return [
            remote(y_send.at[step, 0], y_recv.at[step, 0], step, 2, neighbours[2]),
            remote(y_send.at[step, 1], y_recv.at[step, 1], step, 3, neighbours[3]),
            remote(y_send.at[step, 0, 1], corner_recv.at[step, 0], step, 4, neighbours[4]),
            remote(y_send.at[step, 1, 1], corner_recv.at[step, 1], step, 5, neighbours[5]),
            remote(y_send.at[step, 1, 2], corner_recv.at[step, 2], step, 6, neighbours[6]),
            remote(y_send.at[step, 0, 2], corner_recv.at[step, 3], step, 7, neighbours[7]),
        ]

    def x_copies(step):
        return [
            remote(
                streamed.at[step, pl.ds(0, 5), pl.ds(row_of(CX - 1, 0), CY), :],
                streamed.at[step, pl.ds(0, 5), pl.ds(LOW_SLAB, CY), :],
                step,
                0,
                neighbours[0],
            ),
            remote(
                streamed.at[step, pl.ds(5, 5), pl.ds(row_of(0, 0), CY), :],
                streamed.at[step, pl.ds(5, 5), pl.ds(HIGH_SLAB, CY), :],
                step,
                1,
                neighbours[1],
            ),
        ]

    phase_copies = [
        remote(
            phases.at[:, 0, pl.ds(row_of(CX - 1, 0), CY), :],
            phases.at[:, 0, pl.ds(LOW_SLAB, CY), :],
            STEPS,
            0,
            neighbours[0],
        ),
        remote(
            phases.at[:, 0, pl.ds(row_of(0, 0), CY), :],
            phases.at[:, 0, pl.ds(HIGH_SLAB, CY), :],
            STEPS,
            1,
            neighbours[1],
        ),
        remote(hy_send.at[0], hy_recv.at[0], STEPS, 2, neighbours[2]),
        remote(hy_send.at[1], hy_recv.at[1], STEPS, 3, neighbours[3]),
        remote(hy_send.at[0], hcorner_recv.at[0], STEPS, 4, neighbours[4]),
        remote(hy_send.at[1], hcorner_recv.at[1], STEPS, 5, neighbours[5]),
        remote(hy_send.at[1], hcorner_recv.at[2], STEPS, 6, neighbours[6]),
        remote(hy_send.at[0], hcorner_recv.at[3], STEPS, 7, neighbours[7]),
    ]
    halo_copies = [y_copies(step) + x_copies(step) for step in range(STEPS)]
    for copy in phase_copies:
        copy.start()
    for copy in halo_copies[0]:
        copy.start()

    tile_send[...] = jnp.where(
        lane == 2 * member,
        tile_in[0, 0],
        jnp.where(lane == 2 * member + 1, tile_in[1, 0], 0),
    )
    tile_recv[member] = tile_send[...]

    def route(source, target, kind, device):
        return pltpu.make_async_remote_copy(
            src_ref=source,
            dst_ref=target,
            send_sem=route_send_sem.at[kind],
            recv_sem=route_recv_sem.at[kind],
            device_id=device,
            device_id_type=MESH,
        )

    def wait_bytes(ref, semaphore):
        pltpu.make_async_copy(ref, ref, semaphore).wait()

    def tell_members(shift, carry):
        route(tile_send, tile_recv.at[member], 2 * STEPS, member_device(shift)[1]).start()
        return carry

    lax.fori_loop(1, member_count, tell_members, 0)

    def update(step, prow, crow, column=None):
        final = step == STEPS - 1
        pstep, cstep = (PITCH, CY) if column is not None else (None, None)

        def rows(offset):
            if pstep is None:
                return pl.ds(prow + offset, 8)
            return pl.ds(prow + offset, 8, stride=pstep)

        cells = pl.ds(crow, 8) if cstep is None else pl.ds(crow, 8, stride=cstep)
        own = phases[step, 0, rows(0), :]
        liquid = own > -0.25
        flow = [current[step, axis, cells, :] for axis in range(3)]
        flow_square = flow[0] * flow[0] + flow[1] * flow[1] + flow[2] * flow[2]
        rest = 1.0 - 1.5 * flow_square
        rest_of = {1.0 / 18.0: rest * (2.0 / 18.0), 1.0 / 36.0: rest * (2.0 / 36.0)}
        density = resident[step, 0, cells, :]
        read = [density]
        totals = [None, None, None]
        exchanged = None
        for component in range(1, 19, 2):
            direction = velocity_table[component]
            weight = weight_table[component]
            offset = PITCH * direction[0] + direction[1]
            projection = dot3(direction, flow)
            both = rest_of[weight] + (9.0 * weight) * (projection * projection)
            along = resident[step, component, cells, :]
            against = resident[step, component + 1, cells, :]
            for sign, reverse in ((1, against), (-1, along)):
                place = component if sign == 1 else component + 1
                pulled = streamed[step, SLOT[place], rows(-sign * offset), :]
                near = phases[step, version_of(sign * direction[2]), rows(-sign * offset), :]
                value = jnp.where(
                    near < -0.25, jnp.where(near < -0.75, reverse, both - reverse), pulled
                )
                share = jnp.minimum(jnp.maximum(own + near, 0.0), 1.0)
                moved = share * (pulled - reverse)
                exchanged = moved if exchanged is None else exchanged + moved
                read.append(value)
            density = density + (read[component] + read[component + 1])
            add_momentum(totals, direction, read[component] - read[component + 1])
        interface = jnp.logical_and(liquid, own < 0.75)
        exchanged = jnp.where(interface, exchanged, 0.0)
        if step > 0:
            exchanged = exchanged + mass[step - 1, cells, :]
        mass[step, cells, :] = exchanged
        deck[step, cells, :] = jnp.where(liquid, density * (1.0 / 3.0), 0.0)
        speed = [totals[0], totals[1], totals[2] - relax_time * gravity]
        speed_square = speed[0] * speed[0] + speed[1] * speed[1] + speed[2] * speed[2]
        base = density - 1.5 * speed_square
        gain = 1.0 / relax_time
        keep = 1.0 - gain

        def put(component, value):
            value = jnp.where(liquid, value, weight_table[component])
            resident[step + 1, component, cells, :] = value
            if final or component == 0:
                return
            value = turned(value, velocity_table[component][2])
            streamed[step + 1, SLOT[component], rows(0), :] = value
            if column is not None:
                side, names = (0, Y_PLUS) if column > 0 else (1, Y_MINUS)
                if component in names:
                    y_send[step + 1, side, names.index(component)] = value

        put(0, (gain * weight_table[0]) * base + keep * read[0])
        base_of = {
            1.0 / 18.0: base * (gain / 18.0),
            1.0 / 36.0: base * (gain / 36.0),
        }
        for component in range(1, 19, 2):
            weight = weight_table[component]
            projection = dot3(velocity_table[component], speed)
            even = base_of[weight] + (4.5 * gain * weight) * (projection * projection)
            odd = (3.0 * gain * weight) * projection
            put(component, (even + odd) + keep * read[component])
            put(component + 1, (even - odd) + keep * read[component + 1])
        if not final:
            after = [totals[0], totals[1], totals[2] - gravity]
            for axis in range(3):
                current[step + 1, axis, cells, :] = jnp.where(liquid, after[axis], 0.0)

    def interior(step):
        def slab(x, carry):
            for y in (1, 7):
                update(step, PITCH * x + PITCH + 8 + y, CY * x + y)
            return carry

        lax.fori_loop(1, CX - 1, slab, 0)

    def y_border(step):
        for y in (0, CY - 1):
            update(step, row_of(0, y), y, column=y)

    def x_border(step):
        def slab(index, carry):
            x = (CX - 1) * (index // 2)
            half = 8 * lax.rem(index, 2)
            update(
                step,
                pl.multiple_of(PITCH * x + PITCH + 8 + half, 8),
                pl.multiple_of(CY * x + half, 8),
            )
            return carry

        lax.fori_loop(0, 4, slab, 0)

    corners = (
        (7, row_of(-1, -1), CX - 1),
        (8, row_of(CX, CY), 0),
        (9, row_of(-1, CY), CX - 1),
        (10, row_of(CX, -1), 0),
    )

    def unpack(step):
        for copy in halo_copies[step]:
            copy.wait_recv()
        for side, (y, names) in enumerate(((-1, Y_PLUS), (CY, Y_MINUS))):
            for place, component in enumerate(names):
                streamed[step, SLOT[component], pl.ds(row_of(0, y), CX, stride=PITCH), :] = y_recv[
                    step, side, place
                ]
        for place, (component, row, x) in enumerate(corners):
            streamed[step, SLOT[component], pl.ds(row, 1), :] = corner_recv[
                step, place, pl.ds(x, 1), :
            ]

    def unpack_phases():
        for copy in phase_copies:
            copy.wait_recv()
        at_west, at_east = gx == 0, gx == gx_count - 1
        at_south, at_north = gy == 0, gy == gy_count - 1

        def one(step, carry):
            for start, edge in ((LOW_SLAB, at_west), (HIGH_SLAB, at_east)):
                for half in (0, 8):
                    rows = pl.ds(start + half, 8)
                    put_phase(step, rows, jnp.where(edge, GAS, phases[step, 0, rows, :]))
            for side, (y, edge) in enumerate(((-1, at_south), (CY, at_north))):
                rows = pl.ds(row_of(0, y), CX, stride=PITCH)
                put_phase(step, rows, jnp.where(edge, GAS, hy_recv[side, step]))
            edges = (
                at_west | at_south,
                at_east | at_north,
                at_west | at_north,
                at_east | at_south,
            )
            for place, (component, row, x) in enumerate(corners):
                code = hcorner_recv[place, step, pl.ds(x, 1), :]
                phases[step, 0, pl.ds(row, 1), :] = jnp.where(edges[place], GAS, code)
            return carry

        lax.fori_loop(0, STEPS, one, 0)

    def find_tiles():
        wait_bytes(tile_recv.at[pl.ds(0, member_count - 1)], route_recv_sem.at[2 * STEPS])
        names = tile_recv[0]
        for place in range(1, member_count):
            names = names + tile_recv[place]
        sublane = lax.broadcasted_iota(jnp.int32, (8, NZ), 0)
        none = 2 * member_count
        for part in range((group_count + 7) // 8):
            wanted = (sublane + 8 * part) * member_count + member
            match = jnp.logical_and(names == wanted, lane < none)
            last = jnp.max(jnp.where(match, lane, -1), axis=1, keepdims=True)
            early = jnp.min(jnp.where(match, lane, none), axis=1, keepdims=True)
            early = jnp.where(early == last, none, early)
            last = jnp.where(last < 0, none, last)
            index_block[0, pl.ds(8 * part, 8), :] = jnp.broadcast_to(last, (8, NZ))
            index_block[1, pl.ds(8 * part, 8), :] = jnp.broadcast_to(early, (8, NZ))
        copy = pltpu.make_async_copy(index_block, index_scalars, local_sem.at[4])
        copy.start()
        copy.wait()

    def widen_weights():
        loads_of[3].wait()
        for part in range(CELLS // 16):
            rows = pl.ds(16 * part, 16)
            weights[rows, :] = weights_packed[rows, :].astype(F32)

    def first_leg(step):
        buffer = first[step]

        def tile(place, carry):
            sums = [None] * 8
            for part in range(8):
                cells = pl.ds(pl.multiple_of(64 * place + 8 * part, 8), 8)
                pressure = deck[step, cells, :].astype(jnp.bfloat16).astype(F32)
                pressure = jnp.broadcast_to(pressure[:, 0:1], (8, NZ))
                for part_of in range(8):
                    term = pressure * weights[cells, pl.ds(NZ * part_of, NZ)]
                    sums[part_of] = term if part == 0 else sums[part_of] + term
            for part_of in range(8):
                buffer[2 * member + place, pl.ds(part_of, 1), :] = jnp.sum(
                    sums[part_of], axis=0, keepdims=True
                )
            return carry

        lax.fori_loop(0, 2, tile, 0)
        own = buffer.at[pl.ds(2 * member, 2)]

        def send(shift, carry):
            route(own, own, step, member_device(shift)[1]).start()
            return carry

        lax.fori_loop(1, member_count, send, 0)

    def second_leg(step):
        buffer = first[step]
        wait_bytes(buffer.at[pl.ds(0, 2 * (member_count - 1))], route_recv_sem.at[step])
        for place in range(group_count):
            second_send[step, place] = (
                buffer[index_scalars[0, place, 0]] + buffer[index_scalars[1, place, 0]]
            )
        second_recv[step, group] = second_send[step, group]

        def send(shift, carry):
            other, device = group_device(shift)
            route(
                second_send.at[step, other],
                second_recv.at[step, group],
                STEPS + step,
                device,
            ).start()
            return carry

        lax.fori_loop(1, group_count, send, 0)

    def collect(step):
        wait_bytes(
            second_recv.at[step, pl.ds(0, group_count - 1)], route_recv_sem.at[STEPS + step]
        )
        total = second_recv[step, 0]
        for place in range(1, group_count):
            total = total + second_recv[step, place]
        for part in range(8):
            loads[pl.ds(step, 1), pl.ds(NZ * part, NZ)] = total[part : part + 1, :]

    for step in range(STEPS):
        first[step][2 * member_count] = jnp.zeros((8, NZ), F32)

    for step in range(STEPS):
        interior(step)
        if step == 0:
            widen_weights()
            unpack_phases()
            find_tiles()
        if step >= 2:
            second_leg(step - 2)
        unpack(step)
        y_border(step)
        if step < STEPS - 1:
            for copy in halo_copies[step + 1][:6]:
                copy.start()
        x_border(step)
        if step < STEPS - 1:
            for copy in halo_copies[step + 1][6:]:
                copy.start()
        first_leg(step)

    results = [
        pltpu.make_async_copy(resident.at[STEPS], pops_out, local_sem.at[5]),
        pltpu.make_async_copy(mass.at[STEPS - 1], mass_out, local_sem.at[6]),
    ]
    for copy in results:
        copy.start()
    second_leg(STEPS - 2)
    for step in range(STEPS - 2):
        collect(step)
    second_leg(STEPS - 1)
    collect(STEPS - 2)
    collect(STEPS - 1)
    result = pltpu.make_async_copy(loads, loads_out, local_sem.at[7])
    result.start()
    for copy in phase_copies:
        copy.wait_send()
    for copies in halo_copies:
        for copy in copies:
            copy.wait_send()
    wait_bytes(tile_recv.at[pl.ds(0, member_count - 1)], route_send_sem.at[2 * STEPS])
    for step in range(STEPS):
        wait_bytes(first[step].at[pl.ds(0, 2 * (member_count - 1))], route_send_sem.at[step])
        wait_bytes(
            second_send.at[step, pl.ds(0, group_count - 1)], route_send_sem.at[STEPS + step]
        )
    for copy in results:
        copy.wait()
    result.wait()


def per_device(gx_count, gy_count, populations, cell_flags, fill_level, tile_block, deck_weights):
    members, groups = 2 * gy_count, gx_count // 2
    whole = pl.BlockSpec(memory_space=pl.ANY)
    pops, mass, loads = pl.pallas_call(
        functools.partial(kernel, gx_count, gy_count),
        out_shape=(
            jax.ShapeDtypeStruct((19, CELLS, NZ), F32),
            jax.ShapeDtypeStruct((CELLS, NZ), F32),
            jax.ShapeDtypeStruct((STEPS, 1024), F32),
        ),
        in_specs=[whole, whole, whole, pl.BlockSpec(memory_space=pltpu.SMEM), whole],
        out_specs=(whole, whole, whole),
        scratch_shapes=[
            pltpu.VMEM((STEPS, 18, ROWS, NZ), F32),
            pltpu.VMEM((STEPS + 1, 19, CELLS, NZ), F32),
            pltpu.VMEM((STEPS, 3, ROWS, NZ), F32),
            pltpu.VMEM((STEPS, 3, CELLS, NZ), F32),
            pltpu.VMEM((STEPS, CELLS, NZ), F32),
            pltpu.VMEM((STEPS, CELLS, NZ), F32),
            pltpu.VMEM((STEPS, CELLS, NZ), jnp.int32),
            pltpu.VMEM((CELLS, NZ), F32),
            pltpu.VMEM((CELLS, 1024), jnp.bfloat16),
            pltpu.VMEM((CELLS, 1024), F32),
            pltpu.VMEM((STEPS, 2, 5, 8, NZ), F32),
            pltpu.VMEM((STEPS, 2, 5, 8, NZ), F32),
            pltpu.VMEM((STEPS, 4, 8, NZ), F32),
            pltpu.VMEM((2, STEPS, 8, NZ), F32),
            pltpu.VMEM((2, STEPS, 8, NZ), F32),
            pltpu.VMEM((4, STEPS, 8, NZ), F32),
            pltpu.VMEM((8, NZ), jnp.int32),
            pltpu.VMEM((members, 8, NZ), jnp.int32),
            pltpu.VMEM((2, 16, NZ), jnp.int32),
            pltpu.SMEM((2, 16, NZ), jnp.int32),
            pltpu.VMEM((2 * members + 1, 8, NZ), F32),
            pltpu.VMEM((2 * members + 1, 8, NZ), F32),
            pltpu.VMEM((2 * members + 1, 8, NZ), F32),
            pltpu.VMEM((2 * members + 1, 8, NZ), F32),
            pltpu.VMEM((STEPS, groups, 8, NZ), F32),
            pltpu.VMEM((STEPS, groups, 8, NZ), F32),
            pltpu.VMEM((STEPS, 1024), F32),
            pltpu.SemaphoreType.DMA((8,)),
            pltpu.SemaphoreType.DMA((STEPS + 1, 8)),
            pltpu.SemaphoreType.DMA((STEPS + 1, 8)),
            pltpu.SemaphoreType.DMA((2 * STEPS + 1,)),
            pltpu.SemaphoreType.DMA((2 * STEPS + 1,)),
        ],
        compiler_params=pltpu.CompilerParams(
            collective_id=0, has_side_effects=True, vmem_limit_bytes=40 * 1024 * 1024
        ),
    )(
        populations.reshape(19, CELLS, NZ),
        cell_flags.reshape(STEPS, CELLS, NZ),
        fill_level.reshape(CELLS, NZ),
        tile_block,
        deck_weights.reshape(CELLS, 1024),
    )
    return (
        pops.reshape(19, CX, CY, NZ),
        mass.reshape(CX, CY, NZ),
        loads.reshape(1, STEPS, 1024),
    )


def solution(mesh):
    placed = (
        P(None, "gx", "gy", None),
        P(None, "gx", "gy", None),
        P("gx", "gy", None),
        P("gx", "gy"),
        P("gx", "gy", None, None),
    )
    return jax.shard_map(
        functools.partial(per_device, mesh.shape["gx"], mesh.shape["gy"]),
        mesh=mesh,
        in_specs=placed,
        out_specs=(P(None, "gx", "gy", None), P("gx", "gy", None), P(("gx", "gy"), None, None)),
        check_vma=False,
    )
```

time: 452 us -> 60.1 us (0.13)
  waiting for transfers between devices: 266 us -> 0 us
  other arithmetic: 90.6 us -> 0 us
  starting transfers between devices: 60.1 us -> 0 us
  Pallas kernels: 0 us -> 52.2 us
  between operations: 17.4 us -> 0.64 us
  local copies, waits for them, and re-layouts: 14.3 us -> 7.04 us
    unnamed x2 -> x0, waiting for transfers between devices: 256 us -> none
    ppermute x16 -> x0, starting transfers between devices: 60.1 us -> none  [the longest x8 43.9 us: with_halo(): lax.ppermute(lax.slice_in_dim(block, block.shape[dim] - width, None, axis...]
    pallas_call x0 -> x1, Pallas kernels: none -> 52.2 us  [per_device(): pl.pallas_call(functools.partial(kernel, gx_count, gy_count), out_shape=(...]
    unnamed x75 -> x0, other arithmetic: 33.7 us -> none
    concatenate x7 -> x0, other arithmetic: 21.2 us -> none  [the longest x4 20.5 us: pad_depth(): return jnp.concatenate([below, block, above], axis=3)]
    add x2 -> x0, other arithmetic: 16.1 us -> none  [the longest x1 12.7 us: per_device(): exchanged_total = exchanged_total + exchanged]
    ppermute x16 -> x0, waiting for transfers between devices: 9.58 us -> none  [the longest x8 5.67 us: with_halo(): lax.ppermute(lax.slice_in_dim(block, block.shape[dim] - width, None, axis...]
    select_n x3 -> x0, other arithmetic: 7.71 us -> none  [the longest x2 6.24 us: advance(): relaxed.append(jnp.where(liquid, updated, lattice_weight))]
  transfers between devices with their start and end apart: 17 -> 0, of which waited for: 11 -> 0; matrix products, arithmetic and copies ran while one was open for 8% -> 0% of each run, Pallas kernels for 0% -> 0%
where the time goes in v1:
time: 60.1 us; the launch traced here: 59.9 us
  Pallas kernels  52.2 us (87%)
  local copies, waits for them, and re-layouts  7.04 us (12%)
  between operations  0.64 us (1%)
    pallas_call x1, Pallas kernels, per_device(): pl.pallas_call(functools.partial(kernel, gx_count, gy_count), out_shape=(...  52.2 us
    unnamed x12, local copies, waits for them, and re-layouts  7.04 us

profile of v1, /device:TPU:1, one launch (start us, length us, event | category | flops | bytes accessed | tf_op | source)
XLA Modules:
  0.0 59.9 jit_solution(14690955863371405005)
XLA Ops:
  0.6 0.7 %copy.8.tile_in = s32[2,1]{1,0:T(2,128)S(1)} copy(s32[2,1]{0,1:T(1,128)} %param.8) | data formatting | bytes 16 | tf_op args[3]
  1.4 0.0 copy-start
  1.4 1.3 %copy-done = f32[19,8,16,128]{3,2,1,0:T(8,128)S(1)} copy-done((f32[19,8,16,128]{3,2,1,0:T(8,128)S(1)}, f32[19,8,16,128]{3,2,1,0:T(8,128)}, u32[]{:S(2)}) %copy-start) | copy-done | bytes 1245208
  2.7 0.0 copy-start.1
  2.7 0.9 %copy-done.1 = s32[4,8,16,128]{3,2,1,0:T(8,128)S(1)} copy-done((s32[4,8,16,128]{3,2,1,0:T(8,128)S(1)}, s32[4,8,16,128]{3,2,1,0:T(8,128)}, u32[]{:S(2)}) %copy-start.1) | copy-done | bytes 262168
  3.6 0.0 copy-start.2
  3.6 0.9 %copy-done.2 = bf16[2,1,64,1024]{3,2,1,0:T(8,128)(2,1)S(1)} copy-done((bf16[2,1,64,1024]{3,2,1,0:T(8,128)(2,1)S(1)}, bf16[2,1,64,1024]{3,2,1,0:T(8,128)(2,1)}, u32[]{:S(2)}) %copy-start.2) | copy-done | bytes 262168
  4.6 0.0 copy-start.3
  4.6 0.8 %copy-done.3 = f32[8,16,128]{2,1,0:T(8,128)S(1)} copy-done((f32[8,16,128]{2,1,0:T(8,128)S(1)}, f32[8,16,128]{2,1,0:T(8,128)}, u32[]{:S(2)}) %copy-start.3) | copy-done | bytes 65560
  5.4 52.2 %shard_map.76 = (f32[19,128,128]{2,1,0:T(8,128)S(1)}, f32[128,128]{1,0:T(8,128)S(1)}, f32[4,1024]{1,0:T(4,128)S(1)}) custom-call(f32[19,128,128]{2,1,0:T(8,128)S(1)} %bitcast.7, s32[4,128,128]{2,1,0:T(8,128)S(1)} %bitcast.9, f32[128,128]{1,0:T(8,128)S(1)} %bitcast.11, s32[2,1]{1,0:T(2,128)S(1)} %copy.8.tile_in, bf16[128,1024]{1,0:T(8,128)(2,1)S(1)} %bitcast.10), custom_call_target="tpu_custom_call" | custom-call | tf_op jit(solution)/shard_map/pallas_call | solution.py:629
  57.6 1.0 %copy.12 = f32[19,8,16,128]{3,2,1,0:T(8,128)} copy(f32[19,8,16,128]{3,2,1,0:T(8,128)S(1)} %bitcast.8) | data formatting | bytes 2490368
  58.6 0.6 %copy.13 = f32[8,16,128]{2,1,0:T(8,128)} copy(f32[8,16,128]{2,1,0:T(8,128)S(1)} %bitcast.12) | data formatting | bytes 131072
  59.3 0.6 %copy.14 = f32[1,4,1024]{2,1,0:T(4,128)} copy(f32[1,4,1024]{2,1,0:T(4,128)S(1)} %bitcast.13) | data formatting | bytes 32768
Async XLA Ops:
  1.4 1.3 %copy-start = (f32[19,8,16,128]{3,2,1,0:T(8,128)S(1)}, f32[19,8,16,128]{3,2,1,0:T(8,128)}, u32[]{:S(2)}) copy-start(f32[19,8,16,128]{3,2,1,0:T(8,128)} %param.5) | copy-start | bytes 3735556
  2.7 0.9 %copy-start.1 = (s32[4,8,16,128]{3,2,1,0:T(8,128)S(1)}, s32[4,8,16,128]{3,2,1,0:T(8,128)}, u32[]{:S(2)}) copy-start(s32[4,8,16,128]{3,2,1,0:T(8,128)} %param.6) | copy-start | bytes 786436
  3.6 0.9 %copy-start.2 = (bf16[2,1,64,1024]{3,2,1,0:T(8,128)(2,1)S(1)}, bf16[2,1,64,1024]{3,2,1,0:T(8,128)(2,1)}, u32[]{:S(2)}) copy-start(bf16[2,1,64,1024]{3,2,1,0:T(8,128)(2,1)} %param.9) | copy-start | bytes 786436
  4.6 0.8 %copy-start.3 = (f32[8,16,128]{2,1,0:T(8,128)S(1)}, f32[8,16,128]{2,1,0:T(8,128)}, u32[]{:S(2)}) copy-start(f32[8,16,128]{2,1,0:T(8,128)} %param.7) | copy-start | bytes 196612

commit v2 on v1

--- a/solution.py
+++ b/solution.py
@@ -47,6 +47,9 @@
 Y_MINUS = (4, 8, 9, 16, 18)
 SLOTS = X_PLUS + X_MINUS + (3, 4, 5, 6, 15, 16, 17, 18)
 SLOT = {component: place for place, component in enumerate(SLOTS)}
+DEEP, WIDE = 8, 4
+SLAB_ROWS = CY + 2 * WIDE
+FIELDS = 24
 FLUID, GAS, WALL = 1.0, -0.5, -1.0
 
 
@@ -86,6 +89,70 @@
             totals[axis] = totals[axis] + difference
         else:
             totals[axis] = totals[axis] - difference
+
+
+def gather(own, flow, resident, pulled_of, near_of, with_mass):
+    flow_square = flow[0] * flow[0] + flow[1] * flow[1] + flow[2] * flow[2]
+    rest = 1.0 - 1.5 * flow_square
+    rest_of = {1.0 / 18.0: rest * (2.0 / 18.0), 1.0 / 36.0: rest * (2.0 / 36.0)}
+    density = resident(0)
+    read = [density]
+    totals = [None, None, None]
+    exchanged = None
+    for component in range(1, 19, 2):
+        direction = velocity_table[component]
+        weight = weight_table[component]
+        projection = dot3(direction, flow)
+        both = rest_of[weight] + (9.0 * weight) * (projection * projection)
+        along = resident(component)
+        against = resident(component + 1)
+        for place, reverse in ((component, against), (component + 1, along)):
+            pulled = pulled_of(place)
+            near = near_of(place)
+            read.append(
+                jnp.where(near < -0.25, jnp.where(near < -0.75, reverse, both - reverse), pulled)
+            )
+            if with_mass:
+                share = jnp.minimum(jnp.maximum(own + near, 0.0), 1.0)
+                moved = share * (pulled - reverse)
+                exchanged = moved if exchanged is None else exchanged + moved
+        density = density + (read[component] + read[component + 1])
+        add_momentum(totals, direction, read[component] - read[component + 1])
+    return read, density, totals, exchanged
+
+
+def relax(read, density, totals, put):
+    speed = [totals[0], totals[1], totals[2] - relax_time * gravity]
+    speed_square = speed[0] * speed[0] + speed[1] * speed[1] + speed[2] * speed[2]
+    base = density - 1.5 * speed_square
+    gain = 1.0 / relax_time
+    keep = 1.0 - gain
+    put(0, (gain * weight_table[0]) * base + keep * read[0])
+    base_of = {1.0 / 18.0: base * (gain / 18.0), 1.0 / 36.0: base * (gain / 36.0)}
+    for component in range(1, 19, 2):
+        weight = weight_table[component]
+        projection = dot3(velocity_table[component], speed)
+        even = base_of[weight] + (4.5 * gain * weight) * (projection * projection)
+        odd = (3.0 * gain * weight) * projection
+        put(component, (even + odd) + keep * read[component])
+        put(component + 1, (even - odd) + keep * read[component + 1])
+
+
+def momentum_after(totals):
+    return [totals[0], totals[1], totals[2] - gravity]
+
+
+def rolled(block, shift):
+    shift = shift % NZ
+    return block if shift == 0 else pltpu.roll(block, shift, block.ndim - 1)
+
+
+def slab_shift(direction):
+    return DEEP * direction[0] + direction[2]
+
+
+def slab_version(direction):
+    return 3 * (direction[0] + 1) + direction[2] + 1
 
 
 def kernel(
@@ -104,7 +171,6 @@
     phases,
     current,
     mass,
-    deck,
     flags,
     fill,
     weights_packed,
@@ -119,10 +185,20 @@
     tile_recv,
     index_block,
     index_scalars,
-    first0,
-    first1,
-    first2,
-    first3,
+    slab,
+    slab_resident,
+    slab_streamed,
+    slab_phases,
+    slab_current,
+    slab_deck,
+    x_pack,
+    y_pack,
+    corner_pack,
+    x_pack_recv,
+    y_pack_recv,
+    corner_pack_recv,
+    tile_scalars,
+    first,
     second_send,
     second_recv,
     loads,
@@ -132,7 +208,6 @@
     route_send_sem,
     route_recv_sem,
 ):
-    first = (first0, first1, first2, first3)
     gx = lax.axis_index("gx")
     gy = lax.axis_index("gy")
     group_count = gx_count // 2
@@ -168,6 +243,7 @@
         pltpu.make_async_copy(fill_in, fill, local_sem.at[1]),
         pltpu.make_async_copy(pops_in, resident.at[0], local_sem.at[2]),
         pltpu.make_async_copy(weights_in, weights_packed, local_sem.at[3]),
+        pltpu.make_async_copy(tile_in, tile_scalars, local_sem.at[8]),
     ]
     for copy in loads_of:
         copy.start()
@@ -253,12 +329,12 @@
 
     def y_copies(step):
         return [
-            remote(y_send.at[step, 0], y_recv.at[step, 0], step, 2, neighbours[2]),
-            remote(y_send.at[step, 1], y_recv.at[step, 1], step, 3, neighbours[3]),
             remote(y_send.at[step, 0, 1], corner_recv.at[step, 0], step, 4, neighbours[4]),
             remote(y_send.at[step, 1, 1], corner_recv.at[step, 1], step, 5, neighbours[5]),
             remote(y_send.at[step, 1, 2], corner_recv.at[step, 2], step, 6, neighbours[6]),
             remote(y_send.at[step, 0, 2], corner_recv.at[step, 3], step, 7, neighbours[7]),
+            remote(y_send.at[step, 0], y_recv.at[step, 0], step, 2, neighbours[2]),
+            remote(y_send.at[step, 1], y_recv.at[step, 1], step, 3, neighbours[3]),
         ]
 
     def x_copies(step):
@@ -302,15 +378,81 @@
         remote(hy_send.at[0], hcorner_recv.at[3], STEPS, 7, neighbours[7]),
     ]
     halo_copies = [y_copies(step) + x_copies(step) for step in range(STEPS)]
+    slab_copies = [
+        remote(x_pack.at[0], x_pack_recv.at[0], STEPS + 1, 0, neighbours[0]),
+        remote(x_pack.at[1], x_pack_recv.at[1], STEPS + 1, 1, neighbours[1]),
+        remote(y_pack.at[0], y_pack_recv.at[0], STEPS + 1, 2, neighbours[2]),
+        remote(y_pack.at[1], y_pack_recv.at[1], STEPS + 1, 3, neighbours[3]),
+        remote(corner_pack.at[0], corner_pack_recv.at[0], STEPS + 1, 4, neighbours[4]),
+        remote(corner_pack.at[1], corner_pack_recv.at[1], STEPS + 1, 5, neighbours[5]),
+        remote(corner_pack.at[2], corner_pack_recv.at[2], STEPS + 1, 6, neighbours[6]),
+        remote(corner_pack.at[3], corner_pack_recv.at[3], STEPS + 1, 7, neighbours[7]),
+    ]
+    for copy in halo_copies[0]:
+        copy.start()
     for copy in phase_copies:
         copy.start()
-    for copy in halo_copies[0]:
+
+    lane4 = lax.broadcasted_iota(jnp.int32, (4, NZ), 1)
+
+    def into_slab(block_of):
+        gathered = None
+        for x in range(CX):
+            block = rolled(block_of(x), DEEP * (x + WIDE))
+            gathered = block if x == 0 else jnp.where(lane >= DEEP * (x + WIDE), block, gathered)
+        return gathered
+
+    def slab_population(component, carry):
+        for half in (0, 8):
+            slab[component, pl.ds(WIDE + half, 8), :] = into_slab(
+                lambda x: resident[0, component, pl.ds(CY * x + half, 8), :]
+            )
+        return carry
+
+    def slab_phase(step, carry):
+        for half in (0, 8):
+            slab[19 + step, pl.ds(WIDE + half, 8), :] = into_slab(
+                lambda x: phases[step, 0, pl.ds(row_of(x, half), 8), :]
+            )
+        return carry
+
+    lax.fori_loop(0, 19, slab_population, 0)
+    lax.fori_loop(0, STEPS, slab_phase, 0)
+    slab[FIELDS - 1] = jnp.zeros((SLAB_ROWS, NZ), F32)
+
+    def pack(part, carry):
+        for half in (0, 1):
+            blocks = [slab[4 * part + j, pl.ds(WIDE + 8 * half, 8), :] for j in range(4)]
+            for side, start in ((0, 64), (1, 32)):
+                packed = rolled(blocks[0], -start)
+                for j in (1, 2, 3):
+                    packed = jnp.where(lane >= 32 * j, rolled(blocks[j], 32 * j - start), packed)
+                x_pack[side, part, pl.ds(8 * half, 8), :] = packed
+            for j in (0, 1):
+                packed = jnp.where(
+                    lane < 64, rolled(blocks[2 * j], -32), rolled(blocks[2 * j + 1], 32)
+                )
+                if half == 1:
+                    y_pack[0, part, pl.ds(4 * j, 4), :] = packed[4:8, :]
+                else:
+                    y_pack[1, part, pl.ds(4 * j, 4), :] = packed[0:4, :]
+        return carry
+
+    lax.fori_loop(0, FIELDS // 4, pack, 0)
+    for part in range(FIELDS // 4):
+        rows = pl.ds(4 * (part % 2), 4)
+        corner_pack[0, part // 2, rows, :] = x_pack[0, part, pl.ds(12, 4), :]
+        corner_pack[1, part // 2, rows, :] = x_pack[1, part, pl.ds(0, 4), :]
+        corner_pack[2, part // 2, rows, :] = x_pack[0, part, pl.ds(0, 4), :]
+        corner_pack[3, part // 2, rows, :] = x_pack[1, part, pl.ds(12, 4), :]
+    for copy in slab_copies:
         copy.start()
 
+    loads_of[4].wait()
     tile_send[...] = jnp.where(
         lane == 2 * member,
-        tile_in[0, 0],
-        jnp.where(lane == 2 * member + 1, tile_in[1, 0], 0),
+        tile_scalars[0, 0],
+        jnp.where(lane == 2 * member + 1, tile_scalars[0, 1], 0),
     )
     tile_recv[member] = tile_send[...]
 
@@ -328,7 +470,7 @@
         pltpu.make_async_copy(ref, ref, semaphore).wait()
 
     def tell_members(shift, carry):
-        route(tile_send, tile_recv.at[member], 2 * STEPS, member_device(shift)[1]).start()
+        route(tile_send, tile_recv.at[member], 0, member_device(shift)[1]).start()
         return carry
 
     lax.fori_loop(1, member_count, tell_members, 0)
@@ -345,46 +487,22 @@
         cells = pl.ds(crow, 8) if cstep is None else pl.ds(crow, 8, stride=cstep)
         own = phases[step, 0, rows(0), :]
         liquid = own > -0.25
-        flow = [current[step, axis, cells, :] for axis in range(3)]
-        flow_square = flow[0] * flow[0] + flow[1] * flow[1] + flow[2] * flow[2]
-        rest = 1.0 - 1.5 * flow_square
-        rest_of = {1.0 / 18.0: rest * (2.0 / 18.0), 1.0 / 36.0: rest * (2.0 / 36.0)}
-        density = resident[step, 0, cells, :]
-        read = [density]
-        totals = [None, None, None]
-        exchanged = None
-        for component in range(1, 19, 2):
-            direction = velocity_table[component]
-            weight = weight_table[component]
-            offset = PITCH * direction[0] + direction[1]
-            projection = dot3(direction, flow)
-            both = rest_of[weight] + (9.0 * weight) * (projection * projection)
-            along = resident[step, component, cells, :]
-            against = resident[step, component + 1, cells, :]
-            for sign, reverse in ((1, against), (-1, along)):
-                place = component if sign == 1 else component + 1
-                pulled = streamed[step, SLOT[place], rows(-sign * offset), :]
-                near = phases[step, version_of(sign * direction[2]), rows(-sign * offset), :]
-                value = jnp.where(
-                    near < -0.25, jnp.where(near < -0.75, reverse, both - reverse), pulled
-                )
-                share = jnp.minimum(jnp.maximum(own + near, 0.0), 1.0)
-                moved = share * (pulled - reverse)
-                exchanged = moved if exchanged is None else exchanged + moved
-                read.append(value)
-            density = density + (read[component] + read[component + 1])
-            add_momentum(totals, direction, read[component] - read[component + 1])
+        offsets = [PITCH * direction[0] + direction[1] for direction in velocity_table]
+        read, density, totals, exchanged = gather(
+            own,
+            [current[step, axis, cells, :] for axis in range(3)],
+            lambda component: resident[step, component, cells, :],
+            lambda component: streamed[step, SLOT[component], rows(-offsets[component]), :],
+            lambda component: phases[
+                step, version_of(velocity_table[component][2]), rows(-offsets[component]), :
+            ],
+            True,
+        )
         interface = jnp.logical_and(liquid, own < 0.75)
         exchanged = jnp.where(interface, exchanged, 0.0)
         if step > 0:
             exchanged = exchanged + mass[step - 1, cells, :]
         mass[step, cells, :] = exchanged
-        deck[step, cells, :] = jnp.where(liquid, density * (1.0 / 3.0), 0.0)
-        speed = [totals[0], totals[1], totals[2] - relax_time * gravity]
-        speed_square = speed[0] * speed[0] + speed[1] * speed[1] + speed[2] * speed[2]
-        base = density - 1.5 * speed_square
-        gain = 1.0 / relax_time
-        keep = 1.0 - gain
 
         def put(component, value):
             value = jnp.where(liquid, value, weight_table[component])
@@ -398,22 +516,10 @@
                 if component in names:
                     y_send[step + 1, side, names.index(component)] = value
 
-        put(0, (gain * weight_table[0]) * base + keep * read[0])
-        base_of = {
-            1.0 / 18.0: base * (gain / 18.0),
-            1.0 / 36.0: base * (gain / 36.0),
-        }
-        for component in range(1, 19, 2):
-            weight = weight_table[component]
-            projection = dot3(velocity_table[component], speed)
-            even = base_of[weight] + (4.5 * gain * weight) * (projection * projection)
-            odd = (3.0 * gain * weight) * projection
-            put(component, (even + odd) + keep * read[component])
-            put(component + 1, (even - odd) + keep * read[component + 1])
+        relax(read, density, totals, put)
         if not final:
-            after = [totals[0], totals[1], totals[2] - gravity]
-            for axis in range(3):
-                current[step + 1, axis, cells, :] = jnp.where(liquid, after[axis], 0.0)
+            for axis, value in enumerate(momentum_after(totals)):
+                current[step + 1, axis, cells, :] = jnp.where(liquid, value, 0.0)
 
     def interior(step):
         def slab(x, carry):
@@ -488,7 +594,7 @@
         lax.fori_loop(0, STEPS, one, 0)
 
     def find_tiles():
-        wait_bytes(tile_recv.at[pl.ds(0, member_count - 1)], route_recv_sem.at[2 * STEPS])
+        wait_bytes(tile_recv.at[pl.ds(0, member_count - 1)], route_recv_sem.at[0])
         names = tile_recv[0]
         for place in range(1, member_count):
             names = names + tile_recv[place]
@@ -513,66 +619,179 @@
             rows = pl.ds(16 * part, 16)
             weights[rows, :] = weights_packed[rows, :].astype(F32)
 
-    def first_leg(step):
-        buffer = first[step]
-
-        def tile(place, carry):
-            sums = [None] * 8
-            for part in range(8):
-                cells = pl.ds(pl.multiple_of(64 * place + 8 * part, 8), 8)
-                pressure = deck[step, cells, :].astype(jnp.bfloat16).astype(F32)
-                pressure = jnp.broadcast_to(pressure[:, 0:1], (8, NZ))
-                for part_of in range(8):
-                    term = pressure * weights[cells, pl.ds(NZ * part_of, NZ)]
-                    sums[part_of] = term if part == 0 else sums[part_of] + term
-            for part_of in range(8):
-                buffer[2 * member + place, pl.ds(part_of, 1), :] = jnp.sum(
-                    sums[part_of], axis=0, keepdims=True
+    def unpack_slab():
+        for copy in slab_copies:
+            copy.wait_recv()
+
+        def fields(part, carry):
+            quarter = pl.ds(4 * lax.rem(part, 2), 4)
+            for j in range(4):
+                field = 4 * part + j
+                for half in (0, 8):
+                    rows = pl.ds(WIDE + half, 8)
+                    low = rolled(x_pack_recv[0, part, pl.ds(half, 8), :], -32 * j)
+                    high = rolled(x_pack_recv[1, part, pl.ds(half, 8), :], 96 - 32 * j)
+                    slab[field, rows, :] = jnp.where(
+                        lane < 32, low, jnp.where(lane >= 96, high, slab[field, rows, :])
+                    )
+                for side, row, west_corner, east_corner in ((0, 0, 0, 3), (1, CY + WIDE, 2, 1)):
+                    middle = rolled(
+                        y_pack_recv[side, part, pl.ds(4 * (j // 2), 4), :], 32 - 64 * (j % 2)
+                    )
+                    low = rolled(corner_pack_recv[west_corner, part // 2, quarter, :], -32 * j)
+                    high = rolled(corner_pack_recv[east_corner, part // 2, quarter, :], 96 - 32 * j)
+                    slab[field, pl.ds(row, 4), :] = jnp.where(
+                        lane4 < 32, low, jnp.where(lane4 >= 96, high, middle)
+                    )
+            return carry
+
+        lax.fori_loop(0, FIELDS // 4, fields, 0)
+        low_lane = jnp.where(gx == 0, DEEP * WIDE, 0)
+        high_lane = jnp.where(gx == gx_count - 1, NZ - DEEP * WIDE, NZ)
+        low_row = jnp.where(gy == 0, WIDE, 0)
+        high_row = jnp.where(gy == gy_count - 1, CY + WIDE, SLAB_ROWS)
+        level = lax.rem(lane, DEEP)
+
+        def ready(block, carry):
+            start = pl.multiple_of(8 * block, 8)
+            cells = pl.ds(start, 8)
+            rows = pl.ds(pl.multiple_of(start + 8, 8), 8)
+            totals = [None, None, None]
+            for component in range(1, 19, 2):
+                direction = velocity_table[component]
+                along = slab[component, cells, :]
+                against = slab[component + 1, cells, :]
+                add_momentum(totals, direction, along - against)
+                shift = slab_shift(direction)
+                slab_streamed[0, SLOT[component], rows, :] = rolled(along, shift)
+                slab_streamed[0, SLOT[component + 1], rows, :] = rolled(against, -shift)
+            for axis in range(3):
+                slab_current[0, axis, cells, :] = totals[axis]
+            row = lax.broadcasted_iota(jnp.int32, (8, NZ), 0) + start
+            inside = jnp.logical_and(
+                jnp.logical_and(lane >= low_lane, lane < high_lane),
+                jnp.logical_and(row >= low_row, row < high_row),
+            )
+            for step in range(STEPS):
+                code = jnp.where(inside, slab[19 + step, cells, :], GAS)
+                for shift_x in (-1, 0, 1):
+                    for shift_z in (-1, 0, 1):
+                        direction = (shift_x, 0, shift_z)
+                        value = rolled(code, slab_shift(direction))
+                        if shift_z == 1:
+                            value = jnp.where(level == 0, WALL, value)
+                        slab_phases[step, slab_version(direction), rows, :] = value
+            return carry
+
+        lax.fori_loop(0, SLAB_ROWS // 8, ready, 0)
+
+    def slab_update(step, start):
+        cells = pl.ds(start, 8)
+
+        def rows(offset):
+            return pl.ds(start + 8 + offset, 8)
+
+        def own_of(component):
+            if step == 0:
+                return slab[component, cells, :]
+            return slab_resident[step - 1, component, cells, :]
+
+        own = slab_phases[step, slab_version((0, 0, 0)), rows(0), :]
+        liquid = own > -0.25
+        read, density, totals, _ = gather(
+            own,
+            [slab_current[step, axis, cells, :] for axis in range(3)],
+            own_of,
+            lambda component: slab_streamed[
+                step, SLOT[component], rows(-velocity_table[component][1]), :
+            ],
+            lambda component: slab_phases[
+                step,
+                slab_version(velocity_table[component]),
+                rows(-velocity_table[component][1]),
+                :,
+            ],
+            False,
+        )
+        slab_deck[step, cells, :] = jnp.where(liquid, density * (1.0 / 3.0), 0.0)
+        if step == STEPS - 1:
+            return
+
+        def put(component, value):
+            value = jnp.where(liquid, value, weight_table[component])
+            slab_resident[step, component, cells, :] = value
+            if component > 0:
+                slab_streamed[step + 1, SLOT[component], rows(0), :] = rolled(
+                    value, slab_shift(velocity_table[component])
                 )
+
+        relax(read, density, totals, put)
+        for axis, value in enumerate(momentum_after(totals)):
+            slab_current[step + 1, axis, cells, :] = jnp.where(liquid, value, 0.0)
+
+    def slab_steps():
+        for step in range(STEPS - 1):
+
+            def block(index, carry, step=step):
+                slab_update(step, pl.multiple_of(8 * index, 8))
+                return carry
+
+            lax.fori_loop(0, SLAB_ROWS // 8, block, 0)
+        for start in (WIDE, WIDE + 8):
+            slab_update(STEPS - 1, start)
+
+    def first_leg():
+        def one(step, carry):
+            for tile in range(2):
+                sums = [None] * 8
+                for part in range(8):
+                    x = 4 * tile + part // 2
+                    cells = pl.ds(64 * tile + 8 * part, 8)
+                    pressure = slab_deck[step, pl.ds(WIDE + 8 * (part % 2), 8), :]
+                    pressure = pressure.astype(jnp.bfloat16).astype(F32)
+                    place = DEEP * (x + WIDE)
+                    pressure = jnp.broadcast_to(pressure[:, place : place + 1], (8, NZ))
+                    for column in range(8):
+                        term = pressure * weights[cells, pl.ds(NZ * column, NZ)]
+                        sums[column] = term if part == 0 else sums[column] + term
+                for column in range(8):
+                    first[2 * member + tile, step, pl.ds(column, 1), :] = jnp.sum(
+                        sums[column], axis=0, keepdims=True
+                    )
             return carry
 
-        lax.fori_loop(0, 2, tile, 0)
-        own = buffer.at[pl.ds(2 * member, 2)]
+        lax.fori_loop(0, STEPS, one, 0)
+        own = first.at[pl.ds(2 * member, 2)]
 
         def send(shift, carry):
-            route(own, own, step, member_device(shift)[1]).start()
+            route(own, own, 1, member_device(shift)[1]).start()
             return carry
 
         lax.fori_loop(1, member_count, send, 0)
 
-    def second_leg(step):
-        buffer = first[step]
-        wait_bytes(buffer.at[pl.ds(0, 2 * (member_count - 1))], route_recv_sem.at[step])
+    def second_leg():
+        wait_bytes(first.at[pl.ds(0, 2 * (member_count - 1))], route_recv_sem.at[1])
         for place in range(group_count):
-            second_send[step, place] = (
-                buffer[index_scalars[0, place, 0]] + buffer[index_scalars[1, place, 0]]
-            )
-        second_recv[step, group] = second_send[step, group]
+            second_send[place] = first[index_scalars[0, place, 0]] + first[index_scalars[1, place, 0]]
+        second_recv[group] = second_send[group]
 
         def send(shift, carry):
             other, device = group_device(shift)
-            route(
-                second_send.at[step, other],
-                second_recv.at[step, group],
-                STEPS + step,
-                device,
-            ).start()
+            route(second_send.at[other], second_recv.at[group], 2, device).start()
             return carry
 
         lax.fori_loop(1, group_count, send, 0)
 
-    def collect(step):
-        wait_bytes(
-            second_recv.at[step, pl.ds(0, group_count - 1)], route_recv_sem.at[STEPS + step]
-        )
-        total = second_recv[step, 0]
-        for place in range(1, group_count):
-            total = total + second_recv[step, place]
-        for part in range(8):
-            loads[pl.ds(step, 1), pl.ds(NZ * part, NZ)] = total[part : part + 1, :]
-
-    for step in range(STEPS):
-        first[step][2 * member_count] = jnp.zeros((8, NZ), F32)
+    def collect():
+        wait_bytes(second_recv.at[pl.ds(0, group_count - 1)], route_recv_sem.at[2])
+        for step in range(STEPS):
+            total = second_recv[0, step]
+            for place in range(1, group_count):
+                total = total + second_recv[place, step]
+            for column in range(8):
+                loads[pl.ds(step, 1), pl.ds(NZ * column, NZ)] = total[column : column + 1, :]
+
+    first[2 * member_count] = jnp.zeros((STEPS, 8, NZ), F32)
 
     for step in range(STEPS):
         interior(step)
@@ -580,8 +799,12 @@
             widen_weights()
             unpack_phases()
             find_tiles()
-        if step >= 2:
-            second_leg(step - 2)
+        if step == 1:
+            unpack_slab()
+            slab_steps()
+            first_leg()
+        if step == 2:
+            second_leg()
         unpack(step)
         y_border(step)
         if step < STEPS - 1:
@@ -591,7 +814,6 @@
         if step < STEPS - 1:
             for copy in halo_copies[step + 1][6:]:
                 copy.start()
-        first_leg(step)
 
     results = [
         pltpu.make_async_copy(resident.at[STEPS], pops_out, local_sem.at[5]),
@@ -599,48 +821,55 @@
     ]
     for copy in results:
         copy.start()
-    second_leg(STEPS - 2)
-    for step in range(STEPS - 2):
-        collect(step)
-    second_leg(STEPS - 1)
-    collect(STEPS - 2)
-    collect(STEPS - 1)
+    collect()
     result = pltpu.make_async_copy(loads, loads_out, local_sem.at[7])
     result.start()
     for copy in phase_copies:
         copy.wait_send()
+    for copy in slab_copies:
+        copy.wait_send()
     for copies in halo_copies:
         for copy in copies:
             copy.wait_send()
-    wait_bytes(tile_recv.at[pl.ds(0, member_count - 1)], route_send_sem.at[2 * STEPS])
-    for step in range(STEPS):
-        wait_bytes(first[step].at[pl.ds(0, 2 * (member_count - 1))], route_send_sem.at[step])
-        wait_bytes(
-            second_send.at[step, pl.ds(0, group_count - 1)], route_send_sem.at[STEPS + step]
-        )
+    wait_bytes(tile_recv.at[pl.ds(0, member_count - 1)], route_send_sem.at[0])
+    wait_bytes(first.at[pl.ds(0, 2 * (member_count - 1))], route_send_sem.at[1])
+    wait_bytes(second_send.at[pl.ds(0, group_count - 1)], route_send_sem.at[2])
     for copy in results:
         copy.wait()
     result.wait()
 
 
+def hand_over(pops, mass, loads, pops_out, mass_out, loads_out, semaphores):
+    copies = [
+        pltpu.make_async_copy(pops, pops_out, semaphores.at[0]),
+        pltpu.make_async_copy(mass, mass_out, semaphores.at[1]),
+        pltpu.make_async_copy(loads, loads_out, semaphores.at[2]),
+    ]
+    for copy in copies:
+        copy.start()
+    for copy in copies:
+        copy.wait()
+
+
 def per_device(gx_count, gy_count, populations, cell_flags, fill_level, tile_block, deck_weights):
     members, groups = 2 * gy_count, gx_count // 2
-    whole = pl.BlockSpec(memory_space=pl.ANY)
+    whole = pl.BlockSpec(memory_space=pltpu.HBM)
+    keep = pl.BlockSpec(memory_space=pl.ANY)
+    placed = functools.partial(pltpu.with_memory_space_constraint, memory_space=pltpu.HBM)
     pops, mass, loads = pl.pallas_call(
         functools.partial(kernel, gx_count, gy_count),
         out_shape=(
-            jax.ShapeDtypeStruct((19, CELLS, NZ), F32),
-            jax.ShapeDtypeStruct((CELLS, NZ), F32),
-            jax.ShapeDtypeStruct((STEPS, 1024), F32),
+            pltpu.VMEM((19, CELLS, NZ), F32),
+            pltpu.VMEM((CELLS, NZ), F32),
+            pltpu.VMEM((STEPS, 1024), F32),
         ),
-        in_specs=[whole, whole, whole, pl.BlockSpec(memory_space=pltpu.SMEM), whole],
-        out_specs=(whole, whole, whole),
+        in_specs=[whole] * 5,
+        out_specs=(keep, keep, keep),
         scratch_shapes=[
             pltpu.VMEM((STEPS, 18, ROWS, NZ), F32),
             pltpu.VMEM((STEPS + 1, 19, CELLS, NZ), F32),
             pltpu.VMEM((STEPS, 3, ROWS, NZ), F32),
             pltpu.VMEM((STEPS, 3, CELLS, NZ), F32),
-            pltpu.VMEM((STEPS, CELLS, NZ), F32),
             pltpu.VMEM((STEPS, CELLS, NZ), F32),
             pltpu.VMEM((STEPS, CELLS, NZ), jnp.int32),
             pltpu.VMEM((CELLS, NZ), F32),
@@ -656,29 +885,50 @@
             pltpu.VMEM((members, 8, NZ), jnp.int32),
             pltpu.VMEM((2, 16, NZ), jnp.int32),
             pltpu.SMEM((2, 16, NZ), jnp.int32),
-            pltpu.VMEM((2 * members + 1, 8, NZ), F32),
-            pltpu.VMEM((2 * members + 1, 8, NZ), F32),
-            pltpu.VMEM((2 * members + 1, 8, NZ), F32),
-            pltpu.VMEM((2 * members + 1, 8, NZ), F32),
-            pltpu.VMEM((STEPS, groups, 8, NZ), F32),
-            pltpu.VMEM((STEPS, groups, 8, NZ), F32),
+            pltpu.VMEM((FIELDS, SLAB_ROWS, NZ), F32),
+            pltpu.VMEM((STEPS - 1, 19, SLAB_ROWS, NZ), F32),
+            pltpu.VMEM((STEPS, 18, SLAB_ROWS + 16, NZ), F32),
+            pltpu.VMEM((STEPS, 9, SLAB_ROWS + 16, NZ), F32),
+            pltpu.VMEM((STEPS, 3, SLAB_ROWS, NZ), F32),
+            pltpu.VMEM((STEPS, SLAB_ROWS, NZ), F32),
+            pltpu.VMEM((2, FIELDS // 4, CY, NZ), F32),
+            pltpu.VMEM((2, FIELDS // 4, 8, NZ), F32),
+            pltpu.VMEM((4, FIELDS // 8, 8, NZ), F32),
+            pltpu.VMEM((2, FIELDS // 4, CY, NZ), F32),
+            pltpu.VMEM((2, FIELDS // 4, 8, NZ), F32),
+            pltpu.VMEM((4, FIELDS // 8, 8, NZ), F32),
+            pltpu.SMEM((1, 2), jnp.int32),
+            pltpu.VMEM((2 * members + 1, STEPS, 8, NZ), F32),
+            pltpu.VMEM((groups, STEPS, 8, NZ), F32),
+            pltpu.VMEM((groups, STEPS, 8, NZ), F32),
             pltpu.VMEM((STEPS, 1024), F32),
-            pltpu.SemaphoreType.DMA((8,)),
-            pltpu.SemaphoreType.DMA((STEPS + 1, 8)),
-            pltpu.SemaphoreType.DMA((STEPS + 1, 8)),
-            pltpu.SemaphoreType.DMA((2 * STEPS + 1,)),
-            pltpu.SemaphoreType.DMA((2 * STEPS + 1,)),
+            pltpu.SemaphoreType.DMA((9,)),
+            pltpu.SemaphoreType.DMA((STEPS + 2, 8)),
+            pltpu.SemaphoreType.DMA((STEPS + 2, 8)),
+            pltpu.SemaphoreType.DMA((3,)),
+            pltpu.SemaphoreType.DMA((3,)),
         ],
         compiler_params=pltpu.CompilerParams(
-            collective_id=0, has_side_effects=True, vmem_limit_bytes=40 * 1024 * 1024
+            collective_id=0, has_side_effects=True, vmem_limit_bytes=32 * 1024 * 1024
         ),
     )(
-        populations.reshape(19, CELLS, NZ),
-        cell_flags.reshape(STEPS, CELLS, NZ),
-        fill_level.reshape(CELLS, NZ),
-        tile_block,
-        deck_weights.reshape(CELLS, 1024),
+        placed(populations.reshape(19, CELLS, NZ)),
+        placed(cell_flags.reshape(STEPS, CELLS, NZ)),
+        placed(fill_level.reshape(CELLS, NZ)),
+        placed(tile_block.reshape(1, 2)),
+        placed(deck_weights.reshape(CELLS, 1024)),
     )
+    pops, mass, loads = pl.pallas_call(
+        hand_over,
+        out_shape=(
+            pltpu.HBM((19, CELLS, NZ), F32),
+            pltpu.HBM((CELLS, NZ), F32),
+            pltpu.HBM((STEPS, 1024), F32),
+        ),
+        in_specs=[keep] * 3,
+        out_specs=(whole, whole, whole),
+        scratch_shapes=[pltpu.SemaphoreType.DMA((3,))],
+    )(*(pltpu.with_memory_space_constraint(part, pltpu.VMEM) for part in (pops, mass, loads)))
     return (
         pops.reshape(19, CX, CY, NZ),
         mass.reshape(CX, CY, NZ),

time: 60.1 us -> 51.8 us (0.86)
  local copies, waits for them, and re-layouts: 7.04 us -> 0 us
  Pallas kernels: 52.2 us -> 51.1 us
    unnamed x12 -> x0, local copies, waits for them, and re-layouts: 7.04 us -> none
    pallas_call x1, Pallas kernels: 52.2 us -> 50 us  [per_device(): pl.pallas_call(functools.partial(kernel, gx_count, gy_count), out_shape=(...]
    pallas_call x0 -> x1, Pallas kernels: none -> 1.07 us  [per_device(): pl.pallas_call(hand_over, out_shape=(pltpu.HBM((19, CELLS, NZ), F32), plt...]
where the time goes in v2:
time: 51.8 us; the launch traced here: 51.7 us
  Pallas kernels  51.1 us (99%)
  between operations  0.64 us (1%)
    pallas_call x1, Pallas kernels, per_device(): pl.pallas_call(functools.partial(kernel, gx_count, gy_count), out_shape=(...  50 us
    pallas_call x1, Pallas kernels, per_device(): pl.pallas_call(hand_over, out_shape=(pltpu.HBM((19, CELLS, NZ), F32), plt...  1.07 us

profile of v2, /device:TPU:1, one launch (start us, length us, event | category | flops | bytes accessed | tf_op | source)
XLA Modules:
  0.0 51.7 jit_solution(14703658054552719410)
XLA Ops:
  0.6 50.0 %shard_map.76 = (f32[19,128,128]{2,1,0:T(8,128)S(1)}, f32[128,128]{1,0:T(8,128)S(1)}, f32[4,1024]{1,0:T(4,128)S(1)}) custom-call(f32[19,128,128]{2,1,0:T(8,128)} %bitcast.8, s32[4,128,128]{2,1,0:T(8,128)} %bitcast.9, f32[128,128]{1,0:T(8,128)} %bitcast.11, s32[1,2]{1,0:T(1,128)} %bitcast.12, bf16[128,1024]{1,0:T(8,128)(2,1)} %bitcast.10), custom_call_target="tpu_custom_call" | custom-call | tf_op jit(solution)/shard_map/pallas_call | solution.py:859
  50.7 1.1 %shard_map.77 = (f32[19,128,128]{2,1,0:T(8,128)}, f32[128,128]{1,0:T(8,128)}, f32[4,1024]{1,0:T(4,128)}) custom-call(f32[19,128,128]{2,1,0:T(8,128)S(1)} %get-tuple-element.9.pops, f32[128,128]{1,0:T(8,128)S(1)} %get-tuple-element.10.mass, f32[4,1024]{1,0:T(4,128)S(1)} %get-tuple-element.11.loads), custom_call_target="tpu_custom_call" | custom-call | tf_op jit(solution)/shard_map/pallas_call | solution.py:921

commit v3 on v2

--- a/solution.py
+++ b/solution.py
@@ -51,6 +51,29 @@
 SLAB_ROWS = CY + 2 * WIDE
 FIELDS = 24
 FLUID, GAS, WALL = 1.0, -0.5, -1.0
+
+
+def aligned(value, unit):
+    return value if isinstance(value, int) else pl.multiple_of(value, unit)
+
+
+def remainder(value, unit):
+    return value % unit if isinstance(value, int) else lax.rem(value, unit)
+
+
+def loop(low, high, body, group):
+    if group >= high - low:
+        for index in range(low, high):
+            body(index, 0)
+        return
+    turns = (high - low) // group
+
+    def turn(index, carry):
+        for place in range(group):
+            body(low + index * group + place, 0)
+        return carry
+
+    lax.fori_loop(0, turns, turn, 0)
 
 
 def row_of(x, y):
@@ -180,6 +203,7 @@
     corner_recv,
     hy_send,
     hy_recv,
+    hcorner_send,
     hcorner_recv,
     tile_send,
     tile_recv,
@@ -198,10 +222,12 @@
     y_pack_recv,
     corner_pack_recv,
     tile_scalars,
+    partial,
     first,
     second_send,
     second_recv,
-    loads,
+    third_send,
+    third_recv,
     local_sem,
     halo_send_sem,
     halo_recv_sem,
@@ -213,7 +239,8 @@
     group_count = gx_count // 2
     member_count = 2 * gy_count
     group = gx // 2
-    member = lax.rem(gx, 2) * gy_count + gy
+    core = lax.rem(gx, 2)
+    member = core * gy_count + gy
     east = lax.rem(gx + 1, gx_count)
     west = lax.rem(gx + gx_count - 1, gx_count)
     north = lax.rem(gy + 1, gy_count)
@@ -272,9 +299,9 @@
 
     def code_rows(index, carry):
         x = index // 2
-        half = lax.rem(index, 2)
-        cells = pl.ds(pl.multiple_of(8 * index, 8), 8)
-        rows = pl.ds(pl.multiple_of(PITCH * x + 32 + 8 * half, 8), 8)
+        half = remainder(index, 2)
+        cells = pl.ds(aligned(8 * index, 8), 8)
+        rows = pl.ds(aligned(PITCH * x + 32 + 8 * half, 8), 8)
         level = 0.5 * fill[cells, :]
         for step in range(STEPS):
             kind = flags[step, cells, :]
@@ -284,18 +311,20 @@
             put_phase(step, rows, code)
         return carry
 
-    lax.fori_loop(0, 2 * CX, code_rows, 0)
+    loop(0, 2 * CX, code_rows, 2)
     for step in range(STEPS):
         hy_send[0, step] = phases[step, 0, pl.ds(row_of(0, CY - 1), CX, stride=PITCH), :]
         hy_send[1, step] = phases[step, 0, pl.ds(row_of(0, 0), CX, stride=PITCH), :]
+        for place, (x, y) in enumerate(((CX - 1, CY - 1), (0, 0), (CX - 1, 0), (0, CY - 1))):
+            hcorner_send[place, pl.ds(step, 1), :] = phases[step, 0, pl.ds(row_of(x, y), 1), :]
 
     loads_of[2].wait()
 
     def first_rows(index, carry):
         x = index // 2
-        half = lax.rem(index, 2)
-        cells = pl.ds(pl.multiple_of(8 * index, 8), 8)
-        rows = pl.ds(pl.multiple_of(PITCH * x + 32 + 8 * half, 8), 8)
+        half = remainder(index, 2)
+        cells = pl.ds(aligned(8 * index, 8), 8)
+        rows = pl.ds(aligned(PITCH * x + 32 + 8 * half, 8), 8)
         totals = [None, None, None]
         for component in range(1, 19, 2):
             direction = velocity_table[component]
@@ -308,7 +337,7 @@
             current[0, axis, cells, :] = totals[axis]
         return carry
 
-    lax.fori_loop(0, 2 * CX, first_rows, 0)
+    loop(0, 2 * CX, first_rows, 2)
     for side, (y, components) in enumerate(((CY - 1, Y_PLUS), (0, Y_MINUS))):
         for place, component in enumerate(components):
             y_send[0, side, place] = turned(
@@ -329,10 +358,10 @@
 
     def y_copies(step):
         return [
-            remote(y_send.at[step, 0, 1], corner_recv.at[step, 0], step, 4, neighbours[4]),
-            remote(y_send.at[step, 1, 1], corner_recv.at[step, 1], step, 5, neighbours[5]),
-            remote(y_send.at[step, 1, 2], corner_recv.at[step, 2], step, 6, neighbours[6]),
-            remote(y_send.at[step, 0, 2], corner_recv.at[step, 3], step, 7, neighbours[7]),
+            remote(y_send.at[step, 0, 1, pl.ds(7, 1), :], corner_recv.at[step, 0], step, 4, neighbours[4]),
+            remote(y_send.at[step, 1, 1, pl.ds(0, 1), :], corner_recv.at[step, 1], step, 5, neighbours[5]),
+            remote(y_send.at[step, 1, 2, pl.ds(7, 1), :], corner_recv.at[step, 2], step, 6, neighbours[6]),
+            remote(y_send.at[step, 0, 2, pl.ds(0, 1), :], corner_recv.at[step, 3], step, 7, neighbours[7]),
             remote(y_send.at[step, 0], y_recv.at[step, 0], step, 2, neighbours[2]),
             remote(y_send.at[step, 1], y_recv.at[step, 1], step, 3, neighbours[3]),
         ]
@@ -355,27 +384,34 @@
             ),
         ]
 
-    phase_copies = [
+    def phase_copies_of(part, exchange):
+        start, count = ((0, 1), (1, STEPS - 1))[part]
+        steps = pl.ds(start, count)
+        return [
+            remote(
+                phases.at[steps, 0, pl.ds(row_of(CX - 1, 0), CY), :],
+                phases.at[steps, 0, pl.ds(LOW_SLAB, CY), :],
+                exchange,
+                0,
+                neighbours[0],
+            ),
+            remote(
+                phases.at[steps, 0, pl.ds(row_of(0, 0), CY), :],
+                phases.at[steps, 0, pl.ds(HIGH_SLAB, CY), :],
+                exchange,
+                1,
+                neighbours[1],
+            ),
+            remote(hy_send.at[0, steps], hy_recv.at[0, steps], exchange, 2, neighbours[2]),
+            remote(hy_send.at[1, steps], hy_recv.at[1, steps], exchange, 3, neighbours[3]),
+        ]
+
+    phase_copies = [phase_copies_of(0, STEPS), phase_copies_of(1, STEPS + 2)]
+    phase_copies[0] += [
         remote(
-            phases.at[:, 0, pl.ds(row_of(CX - 1, 0), CY), :],
-            phases.at[:, 0, pl.ds(LOW_SLAB, CY), :],
-            STEPS,
-            0,
-            neighbours[0],
-        ),
-        remote(
-            phases.at[:, 0, pl.ds(row_of(0, 0), CY), :],
-            phases.at[:, 0, pl.ds(HIGH_SLAB, CY), :],
-            STEPS,
-            1,
-            neighbours[1],
-        ),
-        remote(hy_send.at[0], hy_recv.at[0], STEPS, 2, neighbours[2]),
-        remote(hy_send.at[1], hy_recv.at[1], STEPS, 3, neighbours[3]),
-        remote(hy_send.at[0], hcorner_recv.at[0], STEPS, 4, neighbours[4]),
-        remote(hy_send.at[1], hcorner_recv.at[1], STEPS, 5, neighbours[5]),
-        remote(hy_send.at[1], hcorner_recv.at[2], STEPS, 6, neighbours[6]),
-        remote(hy_send.at[0], hcorner_recv.at[3], STEPS, 7, neighbours[7]),
+            hcorner_send.at[place], hcorner_recv.at[place], STEPS, 4 + place, neighbours[4 + place]
+        )
+        for place in range(4)
     ]
     halo_copies = [y_copies(step) + x_copies(step) for step in range(STEPS)]
     slab_copies = [
@@ -390,7 +426,7 @@
     ]
     for copy in halo_copies[0]:
         copy.start()
-    for copy in phase_copies:
+    for copy in phase_copies[0]:
         copy.start()
 
     lane4 = lax.broadcasted_iota(jnp.int32, (4, NZ), 1)
@@ -416,8 +452,8 @@
             )
         return carry
 
-    lax.fori_loop(0, 19, slab_population, 0)
-    lax.fori_loop(0, STEPS, slab_phase, 0)
+    loop(0, 19, slab_population, 19)
+    loop(0, STEPS, slab_phase, STEPS)
     slab[FIELDS - 1] = jnp.zeros((SLAB_ROWS, NZ), F32)
 
     def pack(part, carry):
@@ -438,7 +474,7 @@
                     y_pack[1, part, pl.ds(4 * j, 4), :] = packed[0:4, :]
         return carry
 
-    lax.fori_loop(0, FIELDS // 4, pack, 0)
+    loop(0, FIELDS // 4, pack, FIELDS // 4)
     for part in range(FIELDS // 4):
         rows = pl.ds(4 * (part % 2), 4)
         corner_pack[0, part // 2, rows, :] = x_pack[0, part, pl.ds(12, 4), :]
@@ -446,6 +482,8 @@
         corner_pack[2, part // 2, rows, :] = x_pack[0, part, pl.ds(0, 4), :]
         corner_pack[3, part // 2, rows, :] = x_pack[1, part, pl.ds(12, 4), :]
     for copy in slab_copies:
+        copy.start()
+    for copy in phase_copies[1]:
         copy.start()
 
     loads_of[4].wait()
@@ -502,12 +540,18 @@
         exchanged = jnp.where(interface, exchanged, 0.0)
         if step > 0:
             exchanged = exchanged + mass[step - 1, cells, :]
-        mass[step, cells, :] = exchanged
+        if final:
+            mass_out[cells, :] = exchanged
+        else:
+            mass[step, cells, :] = exchanged
 
         def put(component, value):
             value = jnp.where(liquid, value, weight_table[component])
+            if final:
+                pops_out[component, cells, :] = value
+                return
             resident[step + 1, component, cells, :] = value
-            if final or component == 0:
+            if component == 0:
                 return
             value = turned(value, velocity_table[component][2])
             streamed[step + 1, SLOT[component], rows(0), :] = value
@@ -527,7 +571,7 @@
                 update(step, PITCH * x + PITCH + 8 + y, CY * x + y)
             return carry
 
-        lax.fori_loop(1, CX - 1, slab, 0)
+        loop(1, CX - 1, slab, 1)
 
     def y_border(step):
         for y in (0, CY - 1):
@@ -536,15 +580,15 @@
     def x_border(step):
         def slab(index, carry):
             x = (CX - 1) * (index // 2)
-            half = 8 * lax.rem(index, 2)
+            half = 8 * remainder(index, 2)
             update(
                 step,
-                pl.multiple_of(PITCH * x + PITCH + 8 + half, 8),
-                pl.multiple_of(CY * x + half, 8),
+                aligned(PITCH * x + PITCH + 8 + half, 8),
+                aligned(CY * x + half, 8),
             )
             return carry
 
-        lax.fori_loop(0, 4, slab, 0)
+        loop(0, 4, slab, 4)
 
     corners = (
         (7, row_of(-1, -1), CX - 1),
@@ -562,12 +606,10 @@
                     step, side, place
                 ]
         for place, (component, row, x) in enumerate(corners):
-            streamed[step, SLOT[component], pl.ds(row, 1), :] = corner_recv[
-                step, place, pl.ds(x, 1), :
-            ]
-
-    def unpack_phases():
-        for copy in phase_copies:
+            streamed[step, SLOT[component], pl.ds(row, 1), :] = corner_recv[step, place]
+
+    def unpack_phases(part):
+        for copy in phase_copies[part]:
             copy.wait_recv()
         at_west, at_east = gx == 0, gx == gx_count - 1
         at_south, at_north = gy == 0, gy == gy_count - 1
@@ -587,11 +629,11 @@
                 at_east | at_south,
             )
             for place, (component, row, x) in enumerate(corners):
-                code = hcorner_recv[place, step, pl.ds(x, 1), :]
+                code = hcorner_recv[place, pl.ds(step, 1), :]
                 phases[step, 0, pl.ds(row, 1), :] = jnp.where(edges[place], GAS, code)
             return carry
 
-        lax.fori_loop(0, STEPS, one, 0)
+        loop(*((0, 1), (1, STEPS))[part], one, STEPS)
 
     def find_tiles():
         wait_bytes(tile_recv.at[pl.ds(0, member_count - 1)], route_recv_sem.at[0])
@@ -600,15 +642,18 @@
             names = names + tile_recv[place]
         sublane = lax.broadcasted_iota(jnp.int32, (8, NZ), 0)
         none = 2 * member_count
-        for part in range((group_count + 7) // 8):
-            wanted = (sublane + 8 * part) * member_count + member
+        lasts = earlies = jnp.zeros((8, NZ), jnp.int32)
+        for place in range(group_count):
+            wanted = (2 * place + core) * gy_count + sublane
             match = jnp.logical_and(names == wanted, lane < none)
             last = jnp.max(jnp.where(match, lane, -1), axis=1, keepdims=True)
             early = jnp.min(jnp.where(match, lane, none), axis=1, keepdims=True)
             early = jnp.where(early == last, none, early)
             last = jnp.where(last < 0, none, last)
-            index_block[0, pl.ds(8 * part, 8), :] = jnp.broadcast_to(last, (8, NZ))
-            index_block[1, pl.ds(8 * part, 8), :] = jnp.broadcast_to(early, (8, NZ))
+            lasts = jnp.where(lane == place, last, lasts)
+            earlies = jnp.where(lane == place, early, earlies)
+        index_block[0] = lasts
+        index_block[1] = earlies
         copy = pltpu.make_async_copy(index_block, index_scalars, local_sem.at[4])
         copy.start()
         copy.wait()
@@ -624,7 +669,7 @@
             copy.wait_recv()
 
         def fields(part, carry):
-            quarter = pl.ds(4 * lax.rem(part, 2), 4)
+            quarter = pl.ds(4 * remainder(part, 2), 4)
             for j in range(4):
                 field = 4 * part + j
                 for half in (0, 8):
@@ -645,7 +690,7 @@
                     )
             return carry
 
-        lax.fori_loop(0, FIELDS // 4, fields, 0)
+        loop(0, FIELDS // 4, fields, 6)
         low_lane = jnp.where(gx == 0, DEEP * WIDE, 0)
         high_lane = jnp.where(gx == gx_count - 1, NZ - DEEP * WIDE, NZ)
         low_row = jnp.where(gy == 0, WIDE, 0)
@@ -653,9 +698,9 @@
         level = lax.rem(lane, DEEP)
 
         def ready(block, carry):
-            start = pl.multiple_of(8 * block, 8)
+            start = aligned(8 * block, 8)
             cells = pl.ds(start, 8)
-            rows = pl.ds(pl.multiple_of(start + 8, 8), 8)
+            rows = pl.ds(aligned(start + 8, 8), 8)
             totals = [None, None, None]
             for component in range(1, 19, 2):
                 direction = velocity_table[component]
@@ -683,7 +728,7 @@
                         slab_phases[step, slab_version(direction), rows, :] = value
             return carry
 
-        lax.fori_loop(0, SLAB_ROWS // 8, ready, 0)
+        loop(0, SLAB_ROWS // 8, ready, 3)
 
     def slab_update(step, start):
         cells = pl.ds(start, 8)
@@ -733,10 +778,10 @@
         for step in range(STEPS - 1):
 
             def block(index, carry, step=step):
-                slab_update(step, pl.multiple_of(8 * index, 8))
+                slab_update(step, aligned(8 * index, 8))
                 return carry
 
-            lax.fori_loop(0, SLAB_ROWS // 8, block, 0)
+            loop(0, SLAB_ROWS // 8, block, 3)
         for start in (WIDE, WIDE + 8):
             slab_update(STEPS - 1, start)
 
@@ -755,24 +800,38 @@
                         term = pressure * weights[cells, pl.ds(NZ * column, NZ)]
                         sums[column] = term if part == 0 else sums[column] + term
                 for column in range(8):
-                    first[2 * member + tile, step, pl.ds(column, 1), :] = jnp.sum(
+                    partial[column, tile, pl.ds(step, 1), :] = jnp.sum(
                         sums[column], axis=0, keepdims=True
                     )
             return carry
 
-        lax.fori_loop(0, STEPS, one, 0)
-        own = first.at[pl.ds(2 * member, 2)]
+        loop(0, STEPS, one, 2)
+        for tile in range(2):
+            first[2 * member + tile] = partial[gy, tile]
 
         def send(shift, carry):
-            route(own, own, 1, member_device(shift)[1]).start()
+            other, device = member_device(shift)
+            route(
+                partial.at[lax.rem(other, gy_count)],
+                first.at[pl.ds(2 * member, 2)],
+                1,
+                device,
+            ).start()
             return carry
 
         lax.fori_loop(1, member_count, send, 0)
 
     def second_leg():
         wait_bytes(first.at[pl.ds(0, 2 * (member_count - 1))], route_recv_sem.at[1])
-        for place in range(group_count):
-            second_send[place] = first[index_scalars[0, place, 0]] + first[index_scalars[1, place, 0]]
+
+        def owners(place, carry):
+            for y in range(gy_count):
+                second_send[place, y] = (
+                    first[index_scalars[0, y, place]] + first[index_scalars[1, y, place]]
+                )
+            return carry
+
+        loop(0, group_count, owners, 4)
         second_recv[group] = second_send[group]
 
         def send(shift, carry):
@@ -782,29 +841,47 @@
 
         lax.fori_loop(1, group_count, send, 0)
 
+    def third_leg():
+        wait_bytes(second_recv.at[pl.ds(0, group_count - 1)], route_recv_sem.at[2])
+        for y in range(gy_count):
+            total = second_recv[0, y]
+            for place in range(1, group_count):
+                total = total + second_recv[place, y]
+            third_send[y] = total
+        third_recv[gy] = third_send[gy]
+
+        def send(shift, carry):
+            other = lax.rem(gy + shift, gy_count)
+            route(third_send.at[other], third_recv.at[gy], 3, (gx, other)).start()
+            return carry
+
+        lax.fori_loop(1, gy_count, send, 0)
+
     def collect():
-        wait_bytes(second_recv.at[pl.ds(0, group_count - 1)], route_recv_sem.at[2])
-        for step in range(STEPS):
-            total = second_recv[0, step]
-            for place in range(1, group_count):
-                total = total + second_recv[place, step]
-            for column in range(8):
-                loads[pl.ds(step, 1), pl.ds(NZ * column, NZ)] = total[column : column + 1, :]
-
-    first[2 * member_count] = jnp.zeros((STEPS, 8, NZ), F32)
+        wait_bytes(third_recv.at[pl.ds(0, gy_count - 1)], route_recv_sem.at[3])
+        for y in range(gy_count):
+            loads_out[:, pl.ds(NZ * y, NZ)] = third_recv[y]
+
+    first[2 * member_count] = jnp.zeros((STEPS, NZ), F32)
 
     for step in range(STEPS):
-        interior(step)
         if step == 0:
             widen_weights()
-            unpack_phases()
+            interior(step)
             find_tiles()
+            unpack_phases(0)
         if step == 1:
             unpack_slab()
             slab_steps()
             first_leg()
+            interior(step)
+            unpack_phases(1)
         if step == 2:
+            interior(step)
             second_leg()
+        if step == 3:
+            interior(step)
+            third_leg()
         unpack(step)
         y_border(step)
         if step < STEPS - 1:
@@ -815,17 +892,10 @@
             for copy in halo_copies[step + 1][6:]:
                 copy.start()
 
-    results = [
-        pltpu.make_async_copy(resident.at[STEPS], pops_out, local_sem.at[5]),
-        pltpu.make_async_copy(mass.at[STEPS - 1], mass_out, local_sem.at[6]),
-    ]
-    for copy in results:
-        copy.start()
     collect()
-    result = pltpu.make_async_copy(loads, loads_out, local_sem.at[7])
-    result.start()
-    for copy in phase_copies:
-        copy.wait_send()
+    for copies in phase_copies:
+        for copy in copies:
+            copy.wait_send()
     for copy in slab_copies:
         copy.wait_send()
     for copies in halo_copies:
@@ -834,9 +904,7 @@
     wait_bytes(tile_recv.at[pl.ds(0, member_count - 1)], route_send_sem.at[0])
     wait_bytes(first.at[pl.ds(0, 2 * (member_count - 1))], route_send_sem.at[1])
     wait_bytes(second_send.at[pl.ds(0, group_count - 1)], route_send_sem.at[2])
-    for copy in results:
-        copy.wait()
-    result.wait()
+    wait_bytes(third_send.at[pl.ds(0, gy_count - 1)], route_send_sem.at[3])
 
 
 def hand_over(pops, mass, loads, pops_out, mass_out, loads_out, semaphores):
@@ -864,27 +932,28 @@
             pltpu.VMEM((STEPS, 1024), F32),
         ),
         in_specs=[whole] * 5,
-        out_specs=(keep, keep, keep),
+        out_specs=(pl.BlockSpec(memory_space=pltpu.VMEM),) * 3,
         scratch_shapes=[
             pltpu.VMEM((STEPS, 18, ROWS, NZ), F32),
-            pltpu.VMEM((STEPS + 1, 19, CELLS, NZ), F32),
+            pltpu.VMEM((STEPS, 19, CELLS, NZ), F32),
             pltpu.VMEM((STEPS, 3, ROWS, NZ), F32),
             pltpu.VMEM((STEPS, 3, CELLS, NZ), F32),
-            pltpu.VMEM((STEPS, CELLS, NZ), F32),
+            pltpu.VMEM((STEPS - 1, CELLS, NZ), F32),
             pltpu.VMEM((STEPS, CELLS, NZ), jnp.int32),
             pltpu.VMEM((CELLS, NZ), F32),
             pltpu.VMEM((CELLS, 1024), jnp.bfloat16),
             pltpu.VMEM((CELLS, 1024), F32),
             pltpu.VMEM((STEPS, 2, 5, 8, NZ), F32),
             pltpu.VMEM((STEPS, 2, 5, 8, NZ), F32),
-            pltpu.VMEM((STEPS, 4, 8, NZ), F32),
+            pltpu.VMEM((STEPS, 4, 1, NZ), F32),
             pltpu.VMEM((2, STEPS, 8, NZ), F32),
             pltpu.VMEM((2, STEPS, 8, NZ), F32),
-            pltpu.VMEM((4, STEPS, 8, NZ), F32),
+            pltpu.VMEM((4, STEPS, NZ), F32),
+            pltpu.VMEM((4, STEPS, NZ), F32),
             pltpu.VMEM((8, NZ), jnp.int32),
             pltpu.VMEM((members, 8, NZ), jnp.int32),
-            pltpu.VMEM((2, 16, NZ), jnp.int32),
-            pltpu.SMEM((2, 16, NZ), jnp.int32),
+            pltpu.VMEM((2, 8, NZ), jnp.int32),
+            pltpu.SMEM((2, 8, NZ), jnp.int32),
             pltpu.VMEM((FIELDS, SLAB_ROWS, NZ), F32),
             pltpu.VMEM((STEPS - 1, 19, SLAB_ROWS, NZ), F32),
             pltpu.VMEM((STEPS, 18, SLAB_ROWS + 16, NZ), F32),
@@ -898,15 +967,17 @@
             pltpu.VMEM((2, FIELDS // 4, 8, NZ), F32),
             pltpu.VMEM((4, FIELDS // 8, 8, NZ), F32),
             pltpu.SMEM((1, 2), jnp.int32),
-            pltpu.VMEM((2 * members + 1, STEPS, 8, NZ), F32),
-            pltpu.VMEM((groups, STEPS, 8, NZ), F32),
-            pltpu.VMEM((groups, STEPS, 8, NZ), F32),
-            pltpu.VMEM((STEPS, 1024), F32),
+            pltpu.VMEM((8, 2, STEPS, NZ), F32),
+            pltpu.VMEM((2 * members + 1, STEPS, NZ), F32),
+            pltpu.VMEM((groups, gy_count, STEPS, NZ), F32),
+            pltpu.VMEM((groups, gy_count, STEPS, NZ), F32),
+            pltpu.VMEM((gy_count, STEPS, NZ), F32),
+            pltpu.VMEM((gy_count, STEPS, NZ), F32),
             pltpu.SemaphoreType.DMA((9,)),
-            pltpu.SemaphoreType.DMA((STEPS + 2, 8)),
-            pltpu.SemaphoreType.DMA((STEPS + 2, 8)),
-            pltpu.SemaphoreType.DMA((3,)),
-            pltpu.SemaphoreType.DMA((3,)),
+            pltpu.SemaphoreType.DMA((STEPS + 3, 8)),
+            pltpu.SemaphoreType.DMA((STEPS + 3, 8)),
+            pltpu.SemaphoreType.DMA((4,)),
+            pltpu.SemaphoreType.DMA((4,)),
         ],
         compiler_params=pltpu.CompilerParams(
             collective_id=0, has_side_effects=True, vmem_limit_bytes=32 * 1024 * 1024

time: 51.8 us -> 44.8 us (0.86)
  the two profiles are of different devices: /device:TPU:1 before, /device:TPU:6 now
where the time goes in v3:
time: 44.8 us; the launch traced here: 44.7 us
  Pallas kernels  44 us (98%)
  between operations  0.64 us (1%)
    pallas_call x1, Pallas kernels, per_device(): pl.pallas_call(functools.partial(kernel, gx_count, gy_count), out_shape=(...  43 us
    pallas_call x1, Pallas kernels, per_device(): pl.pallas_call(hand_over, out_shape=(pltpu.HBM((19, CELLS, NZ), F32), plt...  1.07 us

profile of v3, /device:TPU:6, one launch (start us, length us, event | category | flops | bytes accessed | tf_op | source)
XLA Modules:
  0.0 44.7 jit_solution(11890848680561469674)
XLA Ops:
  0.6 43.0 %shard_map.76 = (f32[19,128,128]{2,1,0:T(8,128)S(1)}, f32[128,128]{1,0:T(8,128)S(1)}, f32[4,1024]{1,0:T(4,128)S(1)}) custom-call(f32[19,128,128]{2,1,0:T(8,128)} %bitcast.8, s32[4,128,128]{2,1,0:T(8,128)} %bitcast.9, f32[128,128]{1,0:T(8,128)} %bitcast.11, s32[1,2]{1,0:T(1,128)} %bitcast.12, bf16[128,1024]{1,0:T(8,128)(2,1)} %bitcast.10), custom_call_target="tpu_custom_call" | custom-call | tf_op jit(solution)/shard_map/pallas_call | solution.py:927
  43.6 1.1 %shard_map.77 = (f32[19,128,128]{2,1,0:T(8,128)}, f32[128,128]{1,0:T(8,128)}, f32[4,1024]{1,0:T(4,128)}) custom-call(f32[19,128,128]{2,1,0:T(8,128)S(1)} %get-tuple-element.9.pops, f32[128,128]{1,0:T(8,128)S(1)} %get-tuple-element.10.mass, f32[4,1024]{1,0:T(4,128)S(1)} %get-tuple-element.11.loads), custom_call_target="tpu_custom_call" | custom-call | tf_op jit(solution)/shard_map/pallas_call | solution.py:992

commit v4 on v3

--- a/solution.py
+++ b/solution.py
@@ -50,6 +50,8 @@
 DEEP, WIDE = 8, 4
 SLAB_ROWS = CY + 2 * WIDE
 FIELDS = 24
+Z_HIGH, Z_LOW, Y_COUNT = 4, 2, 4
+Z_COUNT = Z_HIGH * Z_LOW
 FLUID, GAS, WALL = 1.0, -0.5, -1.0
 
 
@@ -236,23 +238,44 @@
 ):
     gx = lax.axis_index("gx")
     gy = lax.axis_index("gy")
-    group_count = gx_count // 2
-    member_count = 2 * gy_count
-    group = gx // 2
+    group_count, member_count = Y_COUNT * (gx_count // (2 * Z_HIGH)), 2 * Z_COUNT
     core = lax.rem(gx, 2)
-    member = core * gy_count + gy
+    chip_x, chip_y = gx // (2 * Z_HIGH), gy // Z_LOW
+    chip_z = Z_LOW * lax.rem(gx // 2, Z_HIGH) + lax.rem(gy, Z_LOW)
+    group = chip_x * Y_COUNT + chip_y
+    member = core * Z_COUNT + chip_z
+
+    def device_of(place_x, place_y, place_z, place_core):
+        return (
+            (place_x * Z_HIGH + place_z // Z_LOW) * 2 + place_core,
+            place_y * Z_LOW + lax.rem(place_z, Z_LOW),
+        )
+
     east = lax.rem(gx + 1, gx_count)
     west = lax.rem(gx + gx_count - 1, gx_count)
     north = lax.rem(gy + 1, gy_count)
     south = lax.rem(gy + gy_count - 1, gy_count)
 
     def member_device(shift):
-        other = lax.rem(member + shift, member_count)
-        return other, (2 * group + other // gy_count, lax.rem(other, gy_count))
+        shift_z, shift_core = shift
+        other_z = lax.rem(chip_z + shift_z, Z_COUNT)
+        return other_z, device_of(chip_x, chip_y, other_z, lax.rem(core + shift_core, 2))
 
     def group_device(shift):
-        other = lax.rem(group + shift, group_count)
-        return other, (2 * other + lax.rem(gx, 2), gy)
+        other_x = lax.rem(chip_x + shift[0], group_count // Y_COUNT)
+        other_y = lax.rem(chip_y + shift[1], Y_COUNT)
+        return other_x * Y_COUNT + other_y, device_of(other_x, other_y, chip_z, core)
+
+    def ring(shift, count):
+        return min(shift, count - shift)
+
+    z_shifts = sorted(range(1, Z_COUNT), key=lambda shift: -ring(shift, Z_COUNT))
+    member_shifts = [(shift, flip) for shift in z_shifts for flip in (0, 1)] + [(0, 1)]
+    x_count = group_count // Y_COUNT
+    group_shifts = sorted(
+        [(i, j) for i in range(x_count) for j in range(Y_COUNT) if i or j],
+        key=lambda shift: -(ring(shift[0], x_count) + ring(shift[1], Y_COUNT)),
+    )
 
     neighbours = (
         (east, gy),
@@ -278,11 +301,11 @@
     barrier = pltpu.get_barrier_semaphore()
     for device in neighbours:
         pl.semaphore_signal(barrier, inc=1, device_id=device, device_id_type=MESH)
-    for shift in range(1, member_count):
+    for shift in member_shifts:
         pl.semaphore_signal(
             barrier, inc=1, device_id=member_device(shift)[1], device_id_type=MESH
         )
-    for shift in range(1, group_count):
+    for shift in group_shifts:
         pl.semaphore_signal(
             barrier, inc=1, device_id=group_device(shift)[1], device_id_type=MESH
         )
@@ -311,7 +334,7 @@
             put_phase(step, rows, code)
         return carry
 
-    loop(0, 2 * CX, code_rows, 2)
+    loop(0, 2 * CX, code_rows, 4)
     for step in range(STEPS):
         hy_send[0, step] = phases[step, 0, pl.ds(row_of(0, CY - 1), CX, stride=PITCH), :]
         hy_send[1, step] = phases[step, 0, pl.ds(row_of(0, 0), CX, stride=PITCH), :]
@@ -337,13 +360,65 @@
             current[0, axis, cells, :] = totals[axis]
         return carry
 
-    loop(0, 2 * CX, first_rows, 2)
+    loop(0, 2 * CX, first_rows, 4)
     for side, (y, components) in enumerate(((CY - 1, Y_PLUS), (0, Y_MINUS))):
         for place, component in enumerate(components):
             y_send[0, side, place] = turned(
                 resident[0, component, pl.ds(y, CX, stride=CY), :], velocity_table[component][2]
             )
 
+    lane4 = lax.broadcasted_iota(jnp.int32, (4, NZ), 1)
+
+    def into_slab(block_of):
+        gathered = None
+        for x in range(CX):
+            block = rolled(block_of(x), DEEP * (x + WIDE))
+            gathered = block if x == 0 else jnp.where(lane >= DEEP * (x + WIDE), block, gathered)
+        return gathered
+
+    def slab_population(component, carry):
+        for half in (0, 8):
+            slab[component, pl.ds(WIDE + half, 8), :] = into_slab(
+                lambda x: resident[0, component, pl.ds(CY * x + half, 8), :]
+            )
+        return carry
+
+    def slab_phase(step, carry):
+        for half in (0, 8):
+            slab[19 + step, pl.ds(WIDE + half, 8), :] = into_slab(
+                lambda x: phases[step, 0, pl.ds(row_of(x, half), 8), :]
+            )
+        return carry
+
+    loop(0, 19, slab_population, 19)
+    loop(0, STEPS, slab_phase, 4)
+    slab[FIELDS - 1] = jnp.zeros((SLAB_ROWS, NZ), F32)
+
+    def pack(part, carry):
+        for half in (0, 1):
+            blocks = [slab[4 * part + j, pl.ds(WIDE + 8 * half, 8), :] for j in range(4)]
+            for side, start in ((0, 64), (1, 32)):
+                packed = rolled(blocks[0], -start)
+                for j in (1, 2, 3):
+                    packed = jnp.where(lane >= 32 * j, rolled(blocks[j], 32 * j - start), packed)
+                x_pack[side, part, pl.ds(8 * half, 8), :] = packed
+            for j in (0, 1):
+                packed = jnp.where(
+                    lane < 64, rolled(blocks[2 * j], -32), rolled(blocks[2 * j + 1], 32)
+                )
+                if half == 1:
+                    y_pack[0, part, pl.ds(4 * j, 4), :] = packed[4:8, :]
+                else:
+                    y_pack[1, part, pl.ds(4 * j, 4), :] = packed[0:4, :]
+        return carry
+
+    loop(0, FIELDS // 4, pack, FIELDS // 4)
+    for part in range(FIELDS // 4):
+        rows = pl.ds(4 * (part % 2), 4)
+        corner_pack[0, part // 2, rows, :] = x_pack[0, part, pl.ds(12, 4), :]
+        corner_pack[1, part // 2, rows, :] = x_pack[1, part, pl.ds(0, 4), :]
+        corner_pack[2, part // 2, rows, :] = x_pack[0, part, pl.ds(0, 4), :]
+        corner_pack[3, part // 2, rows, :] = x_pack[1, part, pl.ds(12, 4), :]
     pl.semaphore_wait(barrier, 8 + member_count - 1 + group_count - 1)
 
     def remote(source, target, exchange, place, device):
@@ -415,77 +490,22 @@
     ]
     halo_copies = [y_copies(step) + x_copies(step) for step in range(STEPS)]
     slab_copies = [
+        remote(corner_pack.at[0], corner_pack_recv.at[0], STEPS + 1, 4, neighbours[4]),
+        remote(corner_pack.at[1], corner_pack_recv.at[1], STEPS + 1, 5, neighbours[5]),
+        remote(corner_pack.at[2], corner_pack_recv.at[2], STEPS + 1, 6, neighbours[6]),
+        remote(corner_pack.at[3], corner_pack_recv.at[3], STEPS + 1, 7, neighbours[7]),
         remote(x_pack.at[0], x_pack_recv.at[0], STEPS + 1, 0, neighbours[0]),
         remote(x_pack.at[1], x_pack_recv.at[1], STEPS + 1, 1, neighbours[1]),
         remote(y_pack.at[0], y_pack_recv.at[0], STEPS + 1, 2, neighbours[2]),
         remote(y_pack.at[1], y_pack_recv.at[1], STEPS + 1, 3, neighbours[3]),
-        remote(corner_pack.at[0], corner_pack_recv.at[0], STEPS + 1, 4, neighbours[4]),
-        remote(corner_pack.at[1], corner_pack_recv.at[1], STEPS + 1, 5, neighbours[5]),
-        remote(corner_pack.at[2], corner_pack_recv.at[2], STEPS + 1, 6, neighbours[6]),
-        remote(corner_pack.at[3], corner_pack_recv.at[3], STEPS + 1, 7, neighbours[7]),
     ]
     for copy in halo_copies[0]:
         copy.start()
     for copy in phase_copies[0]:
         copy.start()
 
-    lane4 = lax.broadcasted_iota(jnp.int32, (4, NZ), 1)
-
-    def into_slab(block_of):
-        gathered = None
-        for x in range(CX):
-            block = rolled(block_of(x), DEEP * (x + WIDE))
-            gathered = block if x == 0 else jnp.where(lane >= DEEP * (x + WIDE), block, gathered)
-        return gathered
-
-    def slab_population(component, carry):
-        for half in (0, 8):
-            slab[component, pl.ds(WIDE + half, 8), :] = into_slab(
-                lambda x: resident[0, component, pl.ds(CY * x + half, 8), :]
-            )
-        return carry
-
-    def slab_phase(step, carry):
-        for half in (0, 8):
-            slab[19 + step, pl.ds(WIDE + half, 8), :] = into_slab(
-                lambda x: phases[step, 0, pl.ds(row_of(x, half), 8), :]
-            )
-        return carry
-
-    loop(0, 19, slab_population, 19)
-    loop(0, STEPS, slab_phase, STEPS)
-    slab[FIELDS - 1] = jnp.zeros((SLAB_ROWS, NZ), F32)
-
-    def pack(part, carry):
-        for half in (0, 1):
-            blocks = [slab[4 * part + j, pl.ds(WIDE + 8 * half, 8), :] for j in range(4)]
-            for side, start in ((0, 64), (1, 32)):
-                packed = rolled(blocks[0], -start)
-                for j in (1, 2, 3):
-                    packed = jnp.where(lane >= 32 * j, rolled(blocks[j], 32 * j - start), packed)
-                x_pack[side, part, pl.ds(8 * half, 8), :] = packed
-            for j in (0, 1):
-                packed = jnp.where(
-                    lane < 64, rolled(blocks[2 * j], -32), rolled(blocks[2 * j + 1], 32)
-                )
-                if half == 1:
-                    y_pack[0, part, pl.ds(4 * j, 4), :] = packed[4:8, :]
-                else:
-                    y_pack[1, part, pl.ds(4 * j, 4), :] = packed[0:4, :]
-        return carry
-
-    loop(0, FIELDS // 4, pack, FIELDS // 4)
-    for part in range(FIELDS // 4):
-        rows = pl.ds(4 * (part % 2), 4)
-        corner_pack[0, part // 2, rows, :] = x_pack[0, part, pl.ds(12, 4), :]
-        corner_pack[1, part // 2, rows, :] = x_pack[1, part, pl.ds(0, 4), :]
-        corner_pack[2, part // 2, rows, :] = x_pack[0, part, pl.ds(0, 4), :]
-        corner_pack[3, part // 2, rows, :] = x_pack[1, part, pl.ds(12, 4), :]
     for copy in slab_copies:
         copy.start()
-    for copy in phase_copies[1]:
-        copy.start()
-
     loads_of[4].wait()
     tile_send[...] = jnp.where(
         lane == 2 * member,
@@ -504,14 +524,12 @@
             device_id_type=MESH,
         )
 
+    for shift in member_shifts:
+        route(tile_send, tile_recv.at[member], 0, member_device(shift)[1]).start()
+
+
     def wait_bytes(ref, semaphore):
         pltpu.make_async_copy(ref, ref, semaphore).wait()
-
-    def tell_members(shift, carry):
-        route(tile_send, tile_recv.at[member], 0, member_device(shift)[1]).start()
-        return carry
-
-    lax.fori_loop(1, member_count, tell_members, 0)
 
     def update(step, prow, crow, column=None):
         final = step == STEPS - 1
@@ -644,7 +662,8 @@
         none = 2 * member_count
         lasts = earlies = jnp.zeros((8, NZ), jnp.int32)
         for place in range(group_count):
-            wanted = (2 * place + core) * gy_count + sublane
+            owner_x, owner_y = device_of(place // Y_COUNT, place % Y_COUNT, sublane, core)
+            wanted = owner_x * gy_count + owner_y
             match = jnp.logical_and(names == wanted, lane < none)
             last = jnp.max(jnp.where(match, lane, -1), axis=1, keepdims=True)
             early = jnp.min(jnp.where(match, lane, none), axis=1, keepdims=True)
@@ -807,60 +826,45 @@
 
         loop(0, STEPS, one, 2)
         for tile in range(2):
-            first[2 * member + tile] = partial[gy, tile]
-
-        def send(shift, carry):
-            other, device = member_device(shift)
-            route(
-                partial.at[lax.rem(other, gy_count)],
-                first.at[pl.ds(2 * member, 2)],
-                1,
-                device,
-            ).start()
-            return carry
-
-        lax.fori_loop(1, member_count, send, 0)
+            first[2 * member + tile] = partial[chip_z, tile]
+
+        for shift in member_shifts:
+            other_z, device = member_device(shift)
+            route(partial.at[other_z], first.at[pl.ds(2 * member, 2)], 1, device).start()
 
     def second_leg():
         wait_bytes(first.at[pl.ds(0, 2 * (member_count - 1))], route_recv_sem.at[1])
 
         def owners(place, carry):
-            for y in range(gy_count):
-                second_send[place, y] = (
-                    first[index_scalars[0, y, place]] + first[index_scalars[1, y, place]]
+            for z in range(Z_COUNT):
+                second_send[place, z] = (
+                    first[index_scalars[0, z, place]] + first[index_scalars[1, z, place]]
                 )
             return carry
 
         loop(0, group_count, owners, 4)
         second_recv[group] = second_send[group]
 
-        def send(shift, carry):
+        for shift in group_shifts:
             other, device = group_device(shift)
             route(second_send.at[other], second_recv.at[group], 2, device).start()
-            return carry
-
-        lax.fori_loop(1, group_count, send, 0)
 
     def third_leg():
         wait_bytes(second_recv.at[pl.ds(0, group_count - 1)], route_recv_sem.at[2])
-        for y in range(gy_count):
-            total = second_recv[0, y]
+        for z in range(Z_COUNT):
+            total = second_recv[0, z]
             for place in range(1, group_count):
-                total = total + second_recv[place, y]
-            third_send[y] = total
-        third_recv[gy] = third_send[gy]
-
-        def send(shift, carry):
-            other = lax.rem(gy + shift, gy_count)
-            route(third_send.at[other], third_recv.at[gy], 3, (gx, other)).start()
-            return carry
-
-        lax.fori_loop(1, gy_count, send, 0)
+                total = total + second_recv[place, z]
+            third_send[z] = total
+        third_recv[chip_z] = third_send[chip_z]
+        for shift in z_shifts:
+            other_z, device = member_device((shift, 0))
+            route(third_send.at[other_z], third_recv.at[chip_z], 3, device).start()
 
     def collect():
-        wait_bytes(third_recv.at[pl.ds(0, gy_count - 1)], route_recv_sem.at[3])
-        for y in range(gy_count):
-            loads_out[:, pl.ds(NZ * y, NZ)] = third_recv[y]
+        wait_bytes(third_recv.at[pl.ds(0, Z_COUNT - 1)], route_recv_sem.at[3])
+        for z in range(Z_COUNT):
+            loads_out[:, pl.ds(NZ * z, NZ)] = third_recv[z]
 
     first[2 * member_count] = jnp.zeros((STEPS, NZ), F32)
 
@@ -868,14 +872,16 @@
         if step == 0:
             widen_weights()
             interior(step)
-            find_tiles()
             unpack_phases(0)
+            for copy in phase_copies[1]:
+                copy.start()
         if step == 1:
             unpack_slab()
             slab_steps()
             first_leg()
             interior(step)
             unpack_phases(1)
+            find_tiles()
         if step == 2:
             interior(step)
             second_leg()
@@ -904,7 +910,7 @@
     wait_bytes(tile_recv.at[pl.ds(0, member_count - 1)], route_send_sem.at[0])
     wait_bytes(first.at[pl.ds(0, 2 * (member_count - 1))], route_send_sem.at[1])
     wait_bytes(second_send.at[pl.ds(0, group_count - 1)], route_send_sem.at[2])
-    wait_bytes(third_send.at[pl.ds(0, gy_count - 1)], route_send_sem.at[3])
+    wait_bytes(third_send.at[pl.ds(0, Z_COUNT - 1)], route_send_sem.at[3])
 
 
 def hand_over(pops, mass, loads, pops_out, mass_out, loads_out, semaphores):
@@ -920,7 +926,7 @@
 
 
 def per_device(gx_count, gy_count, populations, cell_flags, fill_level, tile_block, deck_weights):
-    members, groups = 2 * gy_count, gx_count // 2
+    members, groups = 2 * Z_COUNT, Y_COUNT * (gx_count // (2 * Z_HIGH))
     whole = pl.BlockSpec(memory_space=pltpu.HBM)
     keep = pl.BlockSpec(memory_space=pl.ANY)
     placed = functools.partial(pltpu.with_memory_space_constraint, memory_space=pltpu.HBM)
@@ -969,10 +975,10 @@
             pltpu.SMEM((1, 2), jnp.int32),
             pltpu.VMEM((8, 2, STEPS, NZ), F32),
             pltpu.VMEM((2 * members + 1, STEPS, NZ), F32),
-            pltpu.VMEM((groups, gy_count, STEPS, NZ), F32),
-            pltpu.VMEM((groups, gy_count, STEPS, NZ), F32),
-            pltpu.VMEM((gy_count, STEPS, NZ), F32),
-            pltpu.VMEM((gy_count, STEPS, NZ), F32),
+            pltpu.VMEM((groups, Z_COUNT, STEPS, NZ), F32),
+            pltpu.VMEM((groups, Z_COUNT, STEPS, NZ), F32),
+            pltpu.VMEM((Z_COUNT, STEPS, NZ), F32),
+            pltpu.VMEM((Z_COUNT, STEPS, NZ), F32),
             pltpu.SemaphoreType.DMA((9,)),
             pltpu.SemaphoreType.DMA((STEPS + 3, 8)),
             pltpu.SemaphoreType.DMA((STEPS + 3, 8)),

time: 44.8 us -> 38.7 us (0.86)
  the two profiles are of different devices: /device:TPU:6 before, /device:TPU:1 now
where the time goes in v4:
time: 38.7 us; the launch traced here: 38.6 us
  Pallas kernels  38 us (98%)
  between operations  0.64 us (2%)
    pallas_call x1, Pallas kernels, per_device(): pl.pallas_call(functools.partial(kernel, gx_count, gy_count), out_shape=(...  36.9 us
    pallas_call x1, Pallas kernels, per_device(): pl.pallas_call(hand_over, out_shape=(pltpu.HBM((19, CELLS, NZ), F32), plt...  1.07 us

profile of v4, /device:TPU:1, one launch (start us, length us, event | category | flops | bytes accessed | tf_op | source)
XLA Modules:
  0.0 38.6 jit_solution(13612382499151770459)
XLA Ops:
  0.6 36.9 %shard_map.76 = (f32[19,128,128]{2,1,0:T(8,128)S(1)}, f32[128,128]{1,0:T(8,128)S(1)}, f32[4,1024]{1,0:T(4,128)S(1)}) custom-call(f32[19,128,128]{2,1,0:T(8,128)} %bitcast.8, s32[4,128,128]{2,1,0:T(8,128)} %bitcast.9, f32[128,128]{1,0:T(8,128)} %bitcast.11, s32[1,2]{1,0:T(1,128)} %bitcast.12, bf16[128,1024]{1,0:T(8,128)(2,1)} %bitcast.10), custom_call_target="tpu_custom_call" | custom-call | tf_op jit(solution)/shard_map/pallas_call | solution.py:933
  37.6 1.1 %shard_map.77 = (f32[19,128,128]{2,1,0:T(8,128)}, f32[128,128]{1,0:T(8,128)}, f32[4,1024]{1,0:T(4,128)}) custom-call(f32[19,128,128]{2,1,0:T(8,128)S(1)} %get-tuple-element.9.pops, f32[128,128]{1,0:T(8,128)S(1)} %get-tuple-element.10.mass, f32[4,1024]{1,0:T(4,128)S(1)} %get-tuple-element.11.loads), custom_call_target="tpu_custom_call" | custom-call | tf_op jit(solution)/shard_map/pallas_call | solution.py:998
